TPU v7x, 128 devices: a whole 4x4x4 slice. The times are simulated.
128 devices in a mesh: wide: 16 (over x_hi, z, core), narrow: 8 (over x_lo, y).
Axes of the slice: x: 4 (x_hi: 2, x_lo: 2; x = x_hi * 2 + x_lo), y: 4, z: 4, core: 2. Of those that a mesh axis runs over, the one named last changes fastest.
Arguments:
- pair_elements: bfloat16 [2048, 16000], P(('wide', 'narrow')), may hold values from -2.5 to 2.5
- valence_index: int32 [2048], replicated, may hold values from 0 to 2399
- conduction_index: int32 [2048], replicated, may hold values from 0 to 9599
- val_energy: float32 [2400], replicated, may hold values from -12 to -0.5
- cond_energy: float32 [9600], replicated, may hold values from 0.5 to 20
- omegas: float32 [2], replicated, may hold values from 0.2 to 10
Outputs:
- response: float32 [2, 16000, 16000], P(None, 'wide', 'narrow')
All inputs are finite; a program needn't handle non-finite values.
Results may differ from a plain program's by a relative error of at most 0.0028.
Values may be sent and summed in bfloat16 or wider, within the bound.
No kernel may reach another device: no remote copies, remote signals or barrier semaphores. Data moves between devices by JAX's collectives and lax.ppermute only.
A program may use at most 128 MiB of HBM per device.

v0:
```python
import jax
import jax.numpy as jnp
from jax import lax
from jax.sharding import PartitionSpec as P


def lookup(band_index, energies):
    places = lax.broadcasted_iota(jnp.int32, (band_index.shape[0], energies.shape[0]), 1)
    picked = jnp.where(band_index[:, None] == places, energies[None, :], jnp.float32(0.0))
    return jnp.sum(picked, axis=1)


def pair_weights(valence_index, conduction_index, val_energy, cond_energy, omegas):
    count_all = valence_index.shape[0]
    block_rows = 128

    def one_block(indices):
        valence_rows, conduction_rows = indices
        return lookup(conduction_rows, cond_energy) - lookup(valence_rows, val_energy)

    energy_gap = lax.map(
        one_block, (valence_index.reshape(-1, block_rows), conduction_index.reshape(-1, block_rows))
    ).reshape(count_all)
    gap_row = energy_gap[None, :]
    return -4.0 * gap_row / (gap_row * gap_row + omegas[:, None] * omegas[:, None])


def body(pair_elements, valence_index, conduction_index, val_energy, cond_energy, omegas):
    weight = pair_weights(valence_index, conduction_index, val_energy, cond_energy, omegas)
    collected = lax.all_gather(pair_elements, "narrow", axis=0, tiled=True)
    row_block = lax.all_to_all(collected, "wide", split_axis=1, concat_axis=0, tiled=True)
    scaled = (weight[:, :, None] * row_block[None, :, :]).astype(jnp.bfloat16)
    column_rows = lax.all_to_all(pair_elements, "narrow", split_axis=1, concat_axis=0, tiled=True)
    return jnp.einsum(
        "fpr,pc->frc",
        scaled,
        lax.all_gather(column_rows, "wide", axis=0, tiled=True),
        preferred_element_type=jnp.float32,
    )


def solution(mesh):
    return jax.shard_map(
        body,
        mesh=mesh,
        in_specs=(P(("wide", "narrow"), None), P(), P(), P(), P(), P()),
        out_specs=P(None, "wide", "narrow"),
        check_vma=False,
    )
```

profile of v0, /device:TPU:1, one launch (start us, length us, event | category | flops | bytes accessed | tf_op | source)
XLA Modules:
  0.0 219.3 jit_solution(13068159231765438146)
XLA Ops:
  6.5 0.7 all-gather.3.cloned.1.call-update
  7.3 1.9 all_to_all.26
  9.3 0.3 copy.21
  9.6 14.4 %all_to_all.32 = bf16[16,8,2000]{2,0,1:T(8,128)(2,1)S(1)} all-to-all(bf16[16,8,2000]{2,0,1:T(8,128)(2,1)S(1)} %copy.21), channel_id=1, replica_groups=mesh['wide'=16,'narrow'=8] {'narrow'}, dimensions={1} | all-to-all | bytes 1024000 | tf_op jit(solution)/shard_map/all_to_all | solution.py:33
  23.9 1.0 copy.22
  25.0 40.2 %all-gather.3.cloned.1.call-done = bf16[128,16000]{1,0:T(8,128)(2,1)} async-done(((bf16[16,16000]{1,0:T(8,128)(2,1)}), bf16[128,16000]{1,0:T(8,128)(2,1)}) %all-gather.3.cloned.1.call-update) | async-done | bytes 4096016 | tf_op jit(solution)/shard_map/all_gather | solution.py:30
  65.2 6.3 %copy.18 = bf16[128,16000]{0,1:T(8,128)(2,1)} copy(bf16[128,16000]{1,0:T(8,128)(2,1)} %all-gather.3.cloned.1.call-done) | data formatting | bytes 8192000 | tf_op jit(solution)/shard_map/all_gather | solution.py:30
  71.5 7.7 %all-to-all-start = ((bf16[128,16,1000]{0,2,1:T(8,128)(2,1)}), bf16[128,16,1000]{0,2,1:T(8,128)(2,1)}, u32[]{:S(2)}, u32[]{:S(2)}) async-start(bf16[128,16,1000]{0,2,1:T(8,128)(2,1)} %bitcast.27), calls=%async_computation | async-start | bytes 8192000 | tf_op jit(solution)/shard_map/all_to_all | solution.py:31
  79.3 32.3 %while.10 = (s32[]{:T(128)}, f32[16,128]{1,0:T(8,128)S(1)}, s32[16,128]{1,0:T(8,128)}, f32[9600]{0:T(1024)S(1)}, s32[16,128]{1,0:T(8,128)}, /*index=5*/f32[2400]{0:T(1024)S(1)}, s32[]{:T(128)}, s32[]{:T(128)}) while((s32[]{:T(128)}, f32[16,128]{1,0:T(8,128)S(1)}, s32[16,128]{1,0:T(8,128)}, f32[9600]{0:T(1024)S(1)}, s32[16,128]{1,0:T(8,128)}, ...), condition=%wide.region_3.4_spmd, body=%wide.region_0.3_spmd.sunk | while | flops 4607874 | bytes 54757 | solution.py:21
  79.3 0.7 dynamic-slice_bitcast_fusion.3
  80.0 0.8 select_reduce_fusion.4
  80.8 0.4 select_reduce_fusion.5
  81.3 0.7 dynamic-slice_bitcast_fusion.3
  82.0 0.8 select_reduce_fusion.4
  82.8 0.4 select_reduce_fusion.5
  83.3 0.7 dynamic-slice_bitcast_fusion.3
  84.0 0.8 select_reduce_fusion.4
  84.9 0.4 select_reduce_fusion.5
  85.3 0.7 dynamic-slice_bitcast_fusion.3
  86.0 0.8 select_reduce_fusion.4
  86.9 0.4 select_reduce_fusion.5
  87.3 0.7 dynamic-slice_bitcast_fusion.3
  88.1 0.8 select_reduce_fusion.4
  88.9 0.4 select_reduce_fusion.5
  89.4 0.7 dynamic-slice_bitcast_fusion.3
  90.1 0.8 select_reduce_fusion.4
  90.9 0.4 select_reduce_fusion.5
  91.4 0.7 dynamic-slice_bitcast_fusion.3
  92.1 0.8 select_reduce_fusion.4
  92.9 0.4 select_reduce_fusion.5
  93.4 0.7 dynamic-slice_bitcast_fusion.3
  94.1 0.8 select_reduce_fusion.4
  95.0 0.4 select_reduce_fusion.5
  95.4 0.7 dynamic-slice_bitcast_fusion.3
  96.1 0.8 select_reduce_fusion.4
  97.0 0.4 select_reduce_fusion.5
  97.4 0.7 dynamic-slice_bitcast_fusion.3
  98.2 0.8 select_reduce_fusion.4
  99.0 0.4 select_reduce_fusion.5
  99.5 0.7 dynamic-slice_bitcast_fusion.3
  100.2 0.8 select_reduce_fusion.4
  101.0 0.4 select_reduce_fusion.5
  101.5 0.7 dynamic-slice_bitcast_fusion.3
  102.2 0.8 select_reduce_fusion.4
  103.0 0.4 select_reduce_fusion.5
  103.5 0.7 dynamic-slice_bitcast_fusion.3
  104.2 0.8 select_reduce_fusion.4
  105.1 0.4 select_reduce_fusion.5
  105.5 0.7 dynamic-slice_bitcast_fusion.3
  106.2 0.8 select_reduce_fusion.4
  107.1 0.4 select_reduce_fusion.5
  107.5 0.7 dynamic-slice_bitcast_fusion.3
  108.3 0.8 select_reduce_fusion.4
  109.1 0.4 select_reduce_fusion.5
  109.6 0.7 dynamic-slice_bitcast_fusion.3
  110.3 0.8 select_reduce_fusion.4
  111.1 0.4 select_reduce_fusion.5
  111.6 0.1 add_divide_fusion
  111.7 23.8 %all-to-all-done = bf16[128,16,1000]{0,2,1:T(8,128)(2,1)} async-done(((bf16[128,16,1000]{0,2,1:T(8,128)(2,1)}), bf16[128,16,1000]{0,2,1:T(8,128)(2,1)}, u32[]{:S(2)}, u32[]{:S(2)}) %all-to-all-start) | async-done | bytes 4096032 | tf_op jit(solution)/shard_map/all_to_all | solution.py:31
  135.5 5.8 %convert_bitcast_fusion = f32[16,128,1000]{1,2,0:T(8,128)} fusion(bf16[128,16,1000]{0,2,1:T(8,128)(2,1)} %all-to-all-done), kind=kLoop, calls=%fused_computation.10 | loop fusion | flops 2048000 | bytes 12288000 | tf_op jit(solution)/shard_map/convert_element_type | solution.py:32
  141.4 9.2 %copy.19 = f32[16,128,1000]{2,1,0:T(8,128)} copy(f32[16,128,1000]{1,2,0:T(8,128)} %convert_bitcast_fusion) | data formatting | bytes 16384000 | tf_op jit(solution)/shard_map/convert_element_type | solution.py:32
  150.6 9.4 %copy.20 = f32[2048,1000]{0,1:T(8,128)} copy(f32[2048,1000]{1,0:T(8,128)} %bitcast.26) | data formatting | bytes 16384000 | tf_op jit(solution)/shard_map/convert_element_type | solution.py:32
  159.9 28.6 %all-gather.5.cloned.1.call-done = bf16[2048,2000]{0,1:T(8,128)(2,1)} async-done(((bf16[128,2000]{0,1:T(8,128)(2,1)}), bf16[2048,2000]{0,1:T(8,128)(2,1)}) %all-gather.5.cloned.1.call-update) | async-done | bytes 8192016 | tf_op jit(solution)/shard_map/all_gather | solution.py:37
  188.6 23.9 %fusion = f32[2,1000,2000]{2,1,0:T(8,128)} fusion(bf16[2048,2000]{0,1:T(8,128)(2,1)} %all-gather.5.cloned.1.call-done, f32[2048,1000]{0,1:T(8,128)} %copy.20, f32[2,2048]{1,0:T(2,128)S(1)} %add_divide_fusion), kind=kOutput, calls=%fused_computation.8 | convolution fusion | flops 16392192000 | bytes 32400384 | tf_op jit(solution)/shard_map/fpr,pc->frc/dot_general | solution.py:34
  (44 shorter events, 0.8 us)
Async XLA Ops:
  6.5 58.6 %all-gather.3.cloned.1.call-start = ((), (), s32[]{:S(2)}) async-start(), calls=%async_computation.2 | async-start | bytes 4608000 | tf_op jit(solution)/shard_map/all_gather | solution.py:30
  7.3 181.3 %all-gather.5.cloned.1.call-start = ((), (), s32[]{:S(2)}) async-start(), calls=%async_computation.3 | async-start | bytes 8704000 | tf_op jit(solution)/shard_map/all_gather | solution.py:37
  25.0 54.3 %copy-start = (f32[9600]{0:T(1024)S(1)}, f32[9600]{0:T(1024)}, u32[]{:S(2)}) copy-start(f32[9600]{0:T(1024)} %param.12) | copy-start | bytes 115204
  25.0 54.3 %copy-start.1 = (f32[2400]{0:T(1024)S(1)}, f32[2400]{0:T(1024)}, u32[]{:S(2)}) copy-start(f32[2400]{0:T(1024)} %param.11) | copy-start | bytes 28804
  25.0 86.6 %copy-start.2 = (f32[2]{0:T(128)S(1)}, f32[2]{0:T(128)}, u32[]{:S(2)}) copy-start(f32[2]{0:T(128)} %param.13) | copy-start | bytes 28
  71.5 64.0 %all-to-all-start = ((bf16[128,16,1000]{0,2,1:T(8,128)(2,1)}), bf16[128,16,1000]{0,2,1:T(8,128)(2,1)}, u32[]{:S(2)}, u32[]{:S(2)}) async-start(bf16[128,16,1000]{0,2,1:T(8,128)(2,1)} %bitcast.27), calls=%async_computation | async-start | bytes 8192000 | tf_op jit(solution)/shard_map/all_to_all | solution.py:31
Sparse Core Ops, SparseCore 0:
  9.0 56.1 all-gather.2
  67.4 121.0 all-gather.4
where the time goes:
time: 221 us; the launch traced here: 219 us
  waiting for transfers between devices  93.3 us (42%)
  local copies, waits for them, and re-layouts  40.2 us (18%)
  other arithmetic  25.9 us (12%)
  matrix products  23.9 us (11%)
  blocking collectives  14.4 us (7%)
  between operations  13.5 us (6%)
  starting transfers between devices  7.77 us (4%)
    all_gather x1, waiting for transfers between devices, body(): collected = lax.all_gather(pair_elements, 'narrow', axis=0, tiled=True)  40.2 us
    all_gather x1, waiting for transfers between devices, body(): lax.all_gather(column_rows, 'wide', axis=0, tiled=True)  28.6 us
    dot_general x1, matrix products, body(): jnp.einsum('fpr,pc->frc', scaled, lax.all_gather(column_rows, 'wide', axi...  23.9 us
    all_to_all x1, waiting for transfers between devices, body(): lax.all_to_all(collected, 'wide', split_axis=1, concat_axis=0, tiled=True)  23.8 us
    reduce_sum x32, other arithmetic, lookup(): return jnp.sum(picked, axis=1)  19.8 us
    convert_element_type x2, local copies, waits for them, and re-layouts, body(): scaled = (weight[:, :, None] * row_block[None, :, :]).astype(jnp.bfloat16)  18.6 us
    all_to_all x1, blocking collectives, body(): lax.all_to_all(pair_elements, 'narrow', split_axis=1, concat_axis=0, tile...  14.4 us
    eq x16, local copies, waits for them, and re-layouts, lookup(): band_index[:, None] == places  11.5 us
  transfers between devices with their start and end apart: 3, of which 3 were waited for; matrix products, arithmetic and copies ran while one was open for 29% of the time, Pallas kernels for 0%

commit v1 on v0

v1 whole, which is shorter than its diff:
```python
import functools
import jax
import jax.numpy as jnp
from jax import lax
from jax.experimental import pallas as pl
from jax.experimental.pallas import tpu as pltpu
from jax.sharding import Mesh, PartitionSpec as P

ROWS = 1000
COLUMNS = 2000
WIDE, NARROW, OWN = 16, 8, 16
PAIRS = WIDE * NARROW * OWN
KEEP = NARROW * OWN
CHUNK = WIDE * OWN
TILE = 512
PADDED = -(-COLUMNS // TILE) * TILE


def spread(table):
    rows = -(-table.shape[0] // 1024) * 8
    return jnp.pad(table, (0, rows * 128 - table.shape[0])).reshape(rows, 128)


def weights_kernel(valence_ref, conduction_ref, val_ref, cond_ref, omegas_ref, out_ref):
    def lookup(index, table):
        high, low = index // 128, index % 128
        block = lax.broadcasted_iota(jnp.int32, (table.shape[0], PAIRS), 0)
        picked = lax.dot_general(
            table,
            (block == high).astype(jnp.float32),
            (((0,), (0,)), ((), ())),
            precision=lax.Precision.HIGHEST,
            preferred_element_type=jnp.float32,
        )
        lane = lax.broadcasted_iota(jnp.int32, (128, PAIRS), 0)
        return jnp.sum(jnp.where(lane == low, picked, 0.0), axis=0, keepdims=True)

    gap = lookup(conduction_ref[...], cond_ref[...]) - lookup(valence_ref[...], val_ref[...])
    for f in range(2):
        omega = omegas_ref[f]
        out_ref[f : f + 1, :] = -4.0 * gap / (gap * gap + omega * omega)


def pair_weights(valence_index, conduction_index, val_energy, cond_energy, omegas):
    def order(index):
        return index.reshape(WIDE, NARROW, OWN).transpose(1, 0, 2).reshape(1, PAIRS)

    vmem = pl.BlockSpec(memory_space=pltpu.VMEM)
    return pl.pallas_call(
        weights_kernel,
        out_shape=jax.ShapeDtypeStruct((2, PAIRS), jnp.float32),
        in_specs=[vmem] * 4 + [pl.BlockSpec(memory_space=pltpu.SMEM)],
        out_specs=vmem,
        compiler_params=pltpu.CompilerParams(vmem_limit_bytes=24 << 20),
        name="weights",
    )(order(valence_index), order(conduction_index), spread(val_energy), spread(cond_energy), omegas)


def product_kernel(place_ref, weight_ref, rows_ref, *refs):
    blocks = refs[:WIDE]
    out_ref, rows, scaled, columns, rows_sem, block_sem = refs[WIDE:]
    j = pl.program_id(0)

    def row_copy(n):
        return pltpu.make_async_copy(rows_ref.at[n], rows.at[n], rows_sem.at[n])

    def block_copy(k):
        return pltpu.make_async_copy(blocks[k], columns.at[:, place_ref[k]], block_sem.at[k])

    @pl.when(j == 0)
    def _():
        for n in range(NARROW):
            row_copy(n).start()
        for k in range(WIDE):
            block_copy(k).start()
        for n in range(NARROW):
            row_copy(n).wait()
            part = rows[n].astype(jnp.float32)
            for f in range(2):
                lanes = slice(n * CHUNK, (n + 1) * CHUNK)
                scaled[f, :, lanes] = (part * weight_ref[f : f + 1, lanes]).astype(jnp.bfloat16)
        for k in range(WIDE):
            block_copy(k).wait()

    start = pl.multiple_of(j * TILE, TILE)
    right = columns[:, :, :, pl.ds(start, TILE)].reshape(PAIRS, TILE)
    for f in range(2):
        out_ref[f] = jnp.dot(scaled[f], right, preferred_element_type=jnp.float32)


def product(place, weight, rows, blocks):
    any_space = pl.BlockSpec(memory_space=pl.ANY)
    blocks = [b.reshape(NARROW, OWN, PADDED) for b in blocks]
    return pl.pallas_call(
        product_kernel,
        grid=(PADDED // TILE,),
        out_shape=jax.ShapeDtypeStruct((2, ROWS, COLUMNS), jnp.float32),
        in_specs=[pl.BlockSpec(memory_space=pltpu.SMEM), pl.BlockSpec(memory_space=pltpu.VMEM)]
        + [any_space] * (1 + WIDE),
        out_specs=pl.BlockSpec((2, ROWS, TILE), lambda j: (0, 0, j)),
        scratch_shapes=[
            pltpu.VMEM((NARROW, ROWS, CHUNK), jnp.bfloat16),
            pltpu.VMEM((2, ROWS, PAIRS), jnp.bfloat16),
            pltpu.VMEM((NARROW, WIDE, OWN, PADDED), jnp.bfloat16),
            pltpu.SemaphoreType.DMA((NARROW,)),
            pltpu.SemaphoreType.DMA((WIDE,)),
        ],
        compiler_params=pltpu.CompilerParams(vmem_limit_bytes=52 << 20),
        cost_estimate=pl.CostEstimate(
            flops=4 * ROWS * COLUMNS * PAIRS, bytes_accessed=28 << 20, transcendentals=0
        ),
        name="product",
    )(place, weight, rows, *blocks)


def step(value, axis, size, by):
    return lax.ppermute(value, axis, [(i, (i + by) % size) for i in range(size)])


def gather_columns(own):
    xh, z, c = lax.axis_index("xh"), lax.axis_index("z"), lax.axis_index("c")
    other = step(own, "xh", 2, 1)
    near = [own, other]
    up = [step(v, "z", 4, 1) for v in near]
    down = [step(v, "z", 4, -1) for v in near]
    far = [step(up[0], "z", 4, 1), step(down[1], "z", 4, -1)]
    mine = near + up + down + far
    theirs = [step(v, "c", 2, 1) for v in mine]
    places = []
    for core in (c, 1 - c):
        for k, shift in enumerate((0, 0, 3, 3, 1, 1, 2, 2)):
            places.append(((xh + k) % 2 * 4 + (z + shift) % 4) * 2 + core)
    return mine + theirs, jnp.stack(places).astype(jnp.int32)


def body(pair_elements, valence_index, conduction_index, val_energy, cond_energy, omegas):
    weight = pair_weights(valence_index, conduction_index, val_energy, cond_energy, omegas)
    row_part = lax.all_to_all(pair_elements, ("xh", "z", "c"), split_axis=1, concat_axis=0, tiled=True)
    rows = lax.all_gather(row_part.T, ("xl", "y"))
    slices = jnp.pad(pair_elements.reshape(OWN, NARROW, COLUMNS), ((0, 0), (0, 0), (0, PADDED - COLUMNS)))
    column_part = lax.all_to_all(slices.transpose(1, 0, 2), ("xl", "y"), split_axis=0, concat_axis=0, tiled=True)
    blocks, place = gather_columns(column_part)
    return product(place, weight, rows, blocks)


def solution(mesh):
    fine = Mesh(mesh.devices.reshape(2, 4, 2, 2, 4), ("xh", "z", "c", "xl", "y"))
    wide, narrow = ("xh", "z", "c"), ("xl", "y")
    return jax.shard_map(
        body,
        mesh=fine,
        in_specs=(P(wide + narrow, None), P(), P(), P(), P(), P()),
        out_specs=P(None, wide, narrow),
        check_vma=False,
    )
```

time: 221 us -> 147 us (0.67)
  waiting for transfers between devices: 93.3 us -> 34.4 us
  local copies, waits for them, and re-layouts: 40.2 us -> 9.59 us
  Pallas kernels: 0 us -> 27.1 us
  other arithmetic: 25.9 us -> 0 us
  blocking collectives: 14.4 us -> 38.7 us
  matrix products: 23.9 us -> 0 us
  starting transfers between devices: 7.77 us -> 22.7 us
    all_gather x2 -> x1, waiting for transfers between devices: 68.8 us -> 0.02 us  [body(): rows = lax.all_gather(row_part.T, ('xl', 'y'))]
    ppermute x0 -> x15, waiting for transfers between devices: none -> 34.4 us  [step(): lax.ppermute(value, axis, [(i, (i + by) % size) for i in range(size)])]
    pallas_call x0 -> x2, Pallas kernels: none -> 27.1 us  [the longest x1 24.7 us: product(): pl.pallas_call(product_kernel, grid=(PADDED // TILE,), out_shape=jax.Shap...]
    all_to_all x1 -> x2, blocking collectives: 14.4 us -> 38.7 us  [the longest x1 20.4 us: body(): lax.all_to_all(pair_elements, ('xh', 'z', 'c'), split_axis=1, concat_axis...]
    dot_general x1 -> x0, matrix products: 23.9 us -> none  [body(): jnp.einsum('fpr,pc->frc', scaled, lax.all_gather(column_rows, 'wide', axi...]
    all_to_all x1 -> x0, waiting for transfers between devices: 23.8 us -> none  [body(): lax.all_to_all(collected, 'wide', split_axis=1, concat_axis=0, tiled=True)]
    ppermute x0 -> x15, starting transfers between devices: none -> 22.7 us  [step(): lax.ppermute(value, axis, [(i, (i + by) % size) for i in range(size)])]
    reduce_sum x32 -> x0, other arithmetic: 19.8 us -> none  [lookup(): return jnp.sum(picked, axis=1)]
  transfers between devices with their start and end apart: 3 -> 16, of which waited for: 3 -> 4; matrix products, arithmetic and copies ran while one was open for 29% -> 4% of each run, Pallas kernels for 0% -> 2%
where the time goes in v1:
time: 147 us; the launch traced here: 146 us
  blocking collectives  38.7 us (26%)
  waiting for transfers between devices  34.4 us (23%)
  Pallas kernels  27.1 us (18%)
  starting transfers between devices  22.7 us (15%)
  between operations  13.6 us (9%)
  local copies, waits for them, and re-layouts  9.59 us (7%)
    ppermute x15, waiting for transfers between devices, step(): lax.ppermute(value, axis, [(i, (i + by) % size) for i in range(size)])  34.4 us
    pallas_call x1, Pallas kernels, product(): pl.pallas_call(product_kernel, grid=(PADDED // TILE,), out_shape=jax.Shap...  24.7 us
    ppermute x15, starting transfers between devices, step(): lax.ppermute(value, axis, [(i, (i + by) % size) for i in range(size)])  22.7 us
    all_to_all x1, blocking collectives, body(): lax.all_to_all(pair_elements, ('xh', 'z', 'c'), split_axis=1, concat_axis...  20.4 us
    all_to_all x1, blocking collectives, body(): lax.all_to_all(slices.transpose(1, 0, 2), ('xl', 'y'), split_axis=0, conc...  18.4 us
  transfers between devices with their start and end apart: 16, of which 4 were waited for; matrix products, arithmetic and copies ran while one was open for 4% of the time, Pallas kernels for 2%

profile of v1, /device:TPU:1, one launch (start us, length us, event | category | flops | bytes accessed | tf_op | source)
XLA Modules:
  0.0 146.1 jit_solution(12974431779606704943)
XLA Ops:
  6.5 0.0 all-gather.3.cloned.1.call-start
  6.5 2.0 %all_to_all.17 = bf16[16,16,1000]{2,1,0:T(8,128)(2,1)S(1)} reshape(bf16[16,16000]{1,0:T(8,128)(2,1)} %param.6) | data formatting | bytes 1024000 | tf_op jit(solution)/shard_map/all_to_all | solution.py:138
  8.5 0.3 copy.15
  8.8 20.4 %all_to_all.24 = bf16[16,16,1000]{2,0,1:T(8,128)(2,1)S(1)} all-to-all(bf16[16,16,1000]{2,0,1:T(8,128)(2,1)S(1)} %copy.15), channel_id=1, replica_groups=mesh['xh'=2,'z'=4,'c'=2,'xl'=2,'y'=4] {'xh','z','c'}, dimensions={1} | all-to-all | bytes 1024000 | tf_op jit(solution)/shard_map/all_to_all | solution.py:138
  29.2 1.0 copy.16
  30.2 0.0 all-gather.3.cloned.1.call-update
  30.2 1.9 %reshape.30 = bf16[16,8,2000]{2,1,0:T(8,128)(2,1)S(1)} reshape(bf16[16,16000]{1,0:T(8,128)(2,1)} %param.6) | data formatting | bytes 1024000 | tf_op jit(solution)/shard_map/reshape | solution.py:140
  32.2 0.3 copy.17
  32.6 18.4 %all_to_all.25.refs_0_ = bf16[8,16,2048]{2,1,0:T(8,128)(2,1)S(1)} all-to-all(bf16[8,16,2048]{2,1,0:T(8,128)(2,1)S(1)} %pad_bitcast_fusion), channel_id=1, replica_groups=mesh['xh'=2,'z'=4,'c'=2,'xl'=2,'y'=4] {'xl','y'}, dimensions={0} | all-to-all | bytes 1048576 | tf_op jit(solution)/shard_map/all_to_all | solution.py:141
  50.9 0.4 collective-permute-start
  51.3 0.5 collective-permute-start.3
  51.8 1.0 collective-permute-start.1
  52.8 3.4 %collective-permute-start.7 = (bf16[8,16,2048]{2,1,0:T(8,128)(2,1)S(1)}, bf16[8,16,2048]{2,1,0:T(8,128)(2,1)S(1)}, u32[]{:S(2)}, u32[]{:S(2)}) collective-permute-start(bf16[8,16,2048]{2,1,0:T(8,128)(2,1)S(1)} %all_to_all.25.refs_0_), channel_id=1, source_target_pairs={{0,8},{8,0},{1,9},{9,1},{2,10},{10,2},{3,11},{11,3},{4,12},{12,4},... | collective-permute-start | bytes 1572872 | tf_op jit(solution)/shard_map/ppermute | solution.py:117
  56.2 19.5 %collective-permute-done.refs_1_ = bf16[8,16,2048]{2,1,0:T(8,128)(2,1)S(1)} collective-permute-done((bf16[8,16,2048]{2,1,0:T(8,128)(2,1)S(1)}, bf16[8,16,2048]{2,1,0:T(8,128)(2,1)S(1)}, u32[]{:S(2)}, u32[]{:S(2)}) %collective-permute-start) | collective-permute-done | bytes 524320 | tf_op jit(solution)/shard_map/ppermute | solution.py:117
  75.6 1.6 %collective-permute-start.4 = (bf16[8,16,2048]{2,1,0:T(8,128)(2,1)S(1)}, bf16[8,16,2048]{2,1,0:T(8,128)(2,1)S(1)}, u32[]{:S(2)}, u32[]{:S(2)}) collective-permute-start(bf16[8,16,2048]{2,1,0:T(8,128)(2,1)S(1)} %collective-permute-done.refs_1_), channel_id=1, source_target_pairs={{0,48},{16,0},{32,16},{48,32},{1,49},{17,1},{33,17},{49,33},{2,50}... | collective-permute-start | bytes 1572872 | tf_op jit(solution)/shard_map/ppermute | solution.py:117
  77.3 0.0 collective-permute-done.3.refs_4_
  77.3 0.0 copy-start.1
  77.3 3.5 %collective-permute-start.11 = (bf16[8,16,2048]{2,1,0:T(8,128)(2,1)S(1)}, bf16[8,16,2048]{2,1,0:T(8,128)(2,1)S(1)}, u32[]{:S(2)}, u32[]{:S(2)}) collective-permute-start(bf16[8,16,2048]{2,1,0:T(8,128)(2,1)S(1)} %collective-permute-done.3.refs_4_), channel_id=1, source_target_pairs={{0,8},{8,0},{1,9},{9,1},{2,10},{10,2},{3,11},{11,3},{4,12},{12,4},... | collective-permute-start | bytes 1572872 | tf_op jit(solution)/shard_map/ppermute | solution.py:117
  80.8 0.0 collective-permute-done.1.refs_2_
  80.8 0.1 collective-permute-start.9
  80.9 0.6 collective-permute-start.5
  81.4 0.0 collective-permute-done.7.refs_8_
  81.4 0.0 copy-start.2
  81.5 0.1 collective-permute-start.2
  81.5 3.7 %collective-permute-done.4.refs_5_ = bf16[8,16,2048]{2,1,0:T(8,128)(2,1)S(1)} collective-permute-done((bf16[8,16,2048]{2,1,0:T(8,128)(2,1)S(1)}, bf16[8,16,2048]{2,1,0:T(8,128)(2,1)S(1)}, u32[]{:S(2)}, u32[]{:S(2)}) %collective-permute-start.4) | collective-permute-done | bytes 524320 | tf_op jit(solution)/shard_map/ppermute | solution.py:117
  85.3 0.0 copy-start.3
  85.3 3.5 %collective-permute-start.6 = (bf16[8,16,2048]{2,1,0:T(8,128)(2,1)S(1)}, bf16[8,16,2048]{2,1,0:T(8,128)(2,1)}, u32[]{:S(2)}, u32[]{:S(2)}) collective-permute-start(bf16[8,16,2048]{2,1,0:T(8,128)(2,1)S(1)} %collective-permute-done.4.refs_5_), channel_id=1, source_target_pairs={{0,48},{16,0},{32,16},{48,32},{1,49},{17,1},{33,17},{49,33},{2,50}... | collective-permute-start | bytes 1572872 | tf_op jit(solution)/shard_map/ppermute | solution.py:117
  88.8 0.0 collective-permute-done.11.refs_12_
  88.8 0.0 copy-start.4
  88.8 4.3 %collective-permute-start.8 = (bf16[8,16,2048]{2,1,0:T(8,128)(2,1)S(1)}, bf16[8,16,2048]{2,1,0:T(8,128)(2,1)}, u32[]{:S(2)}, u32[]{:S(2)}) collective-permute-start(bf16[8,16,2048]{2,1,0:T(8,128)(2,1)S(1)} %collective-permute-done.refs_1_), channel_id=1, source_target_pairs={{0,8},{8,0},{1,9},{9,1},{2,10},{10,2},{3,11},{11,3},{4,12},{12,4},... | collective-permute-start | bytes 1572872 | tf_op jit(solution)/shard_map/ppermute | solution.py:117
  93.1 0.0 collective-permute-done.9.refs_10_
  93.1 0.0 copy-start.5
  93.1 0.1 collective-permute-start.12
  93.2 2.0 %collective-permute-done.5.refs_6_ = bf16[8,16,2048]{2,1,0:T(8,128)(2,1)} collective-permute-done((bf16[8,16,2048]{2,1,0:T(8,128)(2,1)S(1)}, bf16[8,16,2048]{2,1,0:T(8,128)(2,1)}, u32[]{:S(2)}, u32[]{:S(2)}) %collective-permute-start.5) | collective-permute-done | bytes 524320 | tf_op jit(solution)/shard_map/ppermute | solution.py:117
  95.3 2.1 %collective-permute-start.13 = (bf16[8,16,2048]{2,1,0:T(8,128)(2,1)}, bf16[8,16,2048]{2,1,0:T(8,128)(2,1)}, u32[]{:S(2)}, u32[]{:S(2)}) collective-permute-start(bf16[8,16,2048]{2,1,0:T(8,128)(2,1)} %collective-permute-done.5.refs_6_), channel_id=1, source_target_pairs={{0,8},{8,0},{1,9},{9,1},{2,10},{10,2},{3,11},{11,3},{4,12},{12,4},... | collective-permute-start | bytes 1572872 | tf_op jit(solution)/shard_map/ppermute | solution.py:117
  97.4 9.1 %collective-permute-done.2.refs_3_ = bf16[8,16,2048]{2,1,0:T(8,128)(2,1)} collective-permute-done((bf16[8,16,2048]{2,1,0:T(8,128)(2,1)S(1)}, bf16[8,16,2048]{2,1,0:T(8,128)(2,1)}, u32[]{:S(2)}, u32[]{:S(2)}) %collective-permute-start.2) | collective-permute-done | bytes 524320 | tf_op jit(solution)/shard_map/ppermute | solution.py:117
  106.5 1.3 collective-permute-start.10
  107.7 0.0 collective-permute-done.6.refs_7_
  107.7 0.0 copy-done.4
  107.8 0.3 collective-permute-start.14
  108.0 0.0 copy-done.5
  108.0 0.8 reshape.24
  108.8 0.1 reshape.25.valence_ref
  108.9 0.8 reshape.26
  109.7 0.1 reshape.27.conduction_ref
  109.8 0.7 pad_bitcast_fusion.2.val_ref
  110.5 0.8 pad_bitcast_fusion.1.cond_ref
  111.3 0.0 copy-start
  111.3 0.7 copy-done
  112.0 2.4 %weights.1.weight_ref = f32[2,2048]{1,0:T(2,128)S(1)} custom-call(s32[1,2048]{1,0:T(1,128)S(1)} %reshape.25.valence_ref, s32[1,2048]{1,0:T(1,128)S(1)} %reshape.27.conduction_ref, f32[24,128]{1,0:T(8,128)S(1)} %pad_bitcast_fusion.2.val_ref, f32[80,128]{1,0:T(8,128)S(1)} %pad_bitcast_fusion.1.cond_ref, f32[2]{0:T(128)S(1)} %copy-done), custom_call_target="tpu_custom_call" | custom-call | tf_op jit(solution)/shard_map/weights/pallas_call | solution.py:49
  114.4 0.1 stack.67.place_ref
  114.5 0.0 collective-permute-done.8.refs_9_
  114.5 0.0 collective-permute-done.13.refs_14_
  114.5 0.0 collective-permute-done.12.refs_13_
  114.5 0.0 collective-permute-done.10.refs_11_
  114.5 0.0 collective-permute-done.14.refs_15_
  114.5 0.0 all-gather.3.cloned.1.call-done
  114.6 0.0 copy-done.1
  114.6 0.0 copy-done.2
  114.6 0.0 copy-done.3
  114.6 24.7 %product.1 = f32[2,1000,2000]{2,1,0:T(8,128)} custom-call(s32[16]{0:T(128)S(1)} %stack.67.place_ref, f32[2,2048]{1,0:T(2,128)S(1)} %weights.1.weight_ref, bf16[8,1000,256]{2,1,0:T(8,128)(2,1)} %bitcast.33, bf16[8,16,2048]{2,1,0:T(8,128)(2,1)S(1)} %all_to_all.25.refs_0_, bf16[8,16,2048]{2,1,0:T(8,128)(2,1)S(1)} %collective-permute-done.refs_1_, ...), custom_call_target="tpu_custom_call" | custom-call | flops 16384000000 | bytes 29360128 | tf_op jit(solution)/shard_map/product/pallas_call | solution.py:94
  (3 shorter events, 0.1 us)
Async XLA Ops:
  6.5 108.0 %all-gather.3.cloned.1.call-start = ((), (), s32[]{:S(2)}) async-start(), calls=%async_computation.2 | async-start | bytes 4608000 | tf_op jit(solution)/shard_map/all_gather | solution.py:139
  50.9 24.7 %collective-permute-start = (bf16[8,16,2048]{2,1,0:T(8,128)(2,1)S(1)}, bf16[8,16,2048]{2,1,0:T(8,128)(2,1)S(1)}, u32[]{:S(2)}, u32[]{:S(2)}) collective-permute-start(bf16[8,16,2048]{2,1,0:T(8,128)(2,1)S(1)} %all_to_all.25.refs_0_), channel_id=1, source_target_pairs={{0,64},{64,0},{1,65},{65,1},{2,66},{66,2},{3,67},{67,3},{4,68},{68... | collective-permute-start | bytes 1572872 | tf_op jit(solution)/shard_map/ppermute | solution.py:117
  51.3 26.0 %collective-permute-start.3 = (bf16[8,16,2048]{2,1,0:T(8,128)(2,1)S(1)}, bf16[8,16,2048]{2,1,0:T(8,128)(2,1)S(1)}, u32[]{:S(2)}, u32[]{:S(2)}) collective-permute-start(bf16[8,16,2048]{2,1,0:T(8,128)(2,1)S(1)} %all_to_all.25.refs_0_), channel_id=1, source_target_pairs={{0,48},{16,0},{32,16},{48,32},{1,49},{17,1},{33,17},{49,33},{2,50}... | collective-permute-start | bytes 1572872 | tf_op jit(solution)/shard_map/ppermute | solution.py:117
  51.8 29.0 %collective-permute-start.1 = (bf16[8,16,2048]{2,1,0:T(8,128)(2,1)S(1)}, bf16[8,16,2048]{2,1,0:T(8,128)(2,1)S(1)}, u32[]{:S(2)}, u32[]{:S(2)}) collective-permute-start(bf16[8,16,2048]{2,1,0:T(8,128)(2,1)S(1)} %all_to_all.25.refs_0_), channel_id=1, source_target_pairs={{0,16},{16,32},{32,48},{48,0},{1,17},{17,33},{33,49},{49,1},{2,18}... | collective-permute-start | bytes 1572872 | tf_op jit(solution)/shard_map/ppermute | solution.py:117
  52.8 28.7 %collective-permute-start.7 = (bf16[8,16,2048]{2,1,0:T(8,128)(2,1)S(1)}, bf16[8,16,2048]{2,1,0:T(8,128)(2,1)S(1)}, u32[]{:S(2)}, u32[]{:S(2)}) collective-permute-start(bf16[8,16,2048]{2,1,0:T(8,128)(2,1)S(1)} %all_to_all.25.refs_0_), channel_id=1, source_target_pairs={{0,8},{8,0},{1,9},{9,1},{2,10},{10,2},{3,11},{11,3},{4,12},{12,4},... | collective-permute-start | bytes 1572872 | tf_op jit(solution)/shard_map/ppermute | solution.py:117
  75.6 9.6 %collective-permute-start.4 = (bf16[8,16,2048]{2,1,0:T(8,128)(2,1)S(1)}, bf16[8,16,2048]{2,1,0:T(8,128)(2,1)S(1)}, u32[]{:S(2)}, u32[]{:S(2)}) collective-permute-start(bf16[8,16,2048]{2,1,0:T(8,128)(2,1)S(1)} %collective-permute-done.refs_1_), channel_id=1, source_target_pairs={{0,48},{16,0},{32,16},{48,32},{1,49},{17,1},{33,17},{49,33},{2,50}... | collective-permute-start | bytes 1572872 | tf_op jit(solution)/shard_map/ppermute | solution.py:117
  77.3 37.3 %copy-start.1 = (bf16[8,16,2048]{2,1,0:T(8,128)(2,1)}, bf16[8,16,2048]{2,1,0:T(8,128)(2,1)S(1)}, u32[]{:S(2)}) copy-start(bf16[8,16,2048]{2,1,0:T(8,128)(2,1)S(1)} %collective-permute-done.3.refs_4_) | copy-start | bytes 1572868
  77.3 11.5 %collective-permute-start.11 = (bf16[8,16,2048]{2,1,0:T(8,128)(2,1)S(1)}, bf16[8,16,2048]{2,1,0:T(8,128)(2,1)S(1)}, u32[]{:S(2)}, u32[]{:S(2)}) collective-permute-start(bf16[8,16,2048]{2,1,0:T(8,128)(2,1)S(1)} %collective-permute-done.3.refs_4_), channel_id=1, source_target_pairs={{0,8},{8,0},{1,9},{9,1},{2,10},{10,2},{3,11},{11,3},{4,12},{12,4},... | collective-permute-start | bytes 1572872 | tf_op jit(solution)/shard_map/ppermute | solution.py:117
  80.8 12.3 %collective-permute-start.9 = (bf16[8,16,2048]{2,1,0:T(8,128)(2,1)S(1)}, bf16[8,16,2048]{2,1,0:T(8,128)(2,1)S(1)}, u32[]{:S(2)}, u32[]{:S(2)}) collective-permute-start(bf16[8,16,2048]{2,1,0:T(8,128)(2,1)S(1)} %collective-permute-done.1.refs_2_), channel_id=1, source_target_pairs={{0,8},{8,0},{1,9},{9,1},{2,10},{10,2},{3,11},{11,3},{4,12},{12,4},... | collective-permute-start | bytes 1572872 | tf_op jit(solution)/shard_map/ppermute | solution.py:117
  80.9 14.4 %collective-permute-start.5 = (bf16[8,16,2048]{2,1,0:T(8,128)(2,1)S(1)}, bf16[8,16,2048]{2,1,0:T(8,128)(2,1)}, u32[]{:S(2)}, u32[]{:S(2)}) collective-permute-start(bf16[8,16,2048]{2,1,0:T(8,128)(2,1)S(1)} %collective-permute-done.1.refs_2_), channel_id=1, source_target_pairs={{0,16},{16,32},{32,48},{48,0},{1,17},{17,33},{33,49},{49,1},{2,18}... | collective-permute-start | bytes 1572872 | tf_op jit(solution)/shard_map/ppermute | solution.py:117
  81.4 33.1 %copy-start.2 = (bf16[8,16,2048]{2,1,0:T(8,128)(2,1)}, bf16[8,16,2048]{2,1,0:T(8,128)(2,1)S(1)}, u32[]{:S(2)}) copy-start(bf16[8,16,2048]{2,1,0:T(8,128)(2,1)S(1)} %collective-permute-done.7.refs_8_) | copy-start | bytes 1572868
  81.5 25.0 %collective-permute-start.2 = (bf16[8,16,2048]{2,1,0:T(8,128)(2,1)S(1)}, bf16[8,16,2048]{2,1,0:T(8,128)(2,1)}, u32[]{:S(2)}, u32[]{:S(2)}) collective-permute-start(bf16[8,16,2048]{2,1,0:T(8,128)(2,1)S(1)} %collective-permute-done.refs_1_), channel_id=1, source_target_pairs={{0,16},{16,32},{32,48},{48,0},{1,17},{17,33},{33,49},{49,1},{2,18}... | collective-permute-start | bytes 1572872 | tf_op jit(solution)/shard_map/ppermute | solution.py:117
  85.3 29.3 %copy-start.3 = (bf16[8,16,2048]{2,1,0:T(8,128)(2,1)}, bf16[8,16,2048]{2,1,0:T(8,128)(2,1)S(1)}, u32[]{:S(2)}) copy-start(bf16[8,16,2048]{2,1,0:T(8,128)(2,1)S(1)} %collective-permute-done.4.refs_5_) | copy-start | bytes 1572868
  85.3 22.5 %collective-permute-start.6 = (bf16[8,16,2048]{2,1,0:T(8,128)(2,1)S(1)}, bf16[8,16,2048]{2,1,0:T(8,128)(2,1)}, u32[]{:S(2)}, u32[]{:S(2)}) collective-permute-start(bf16[8,16,2048]{2,1,0:T(8,128)(2,1)S(1)} %collective-permute-done.4.refs_5_), channel_id=1, source_target_pairs={{0,48},{16,0},{32,16},{48,32},{1,49},{17,1},{33,17},{49,33},{2,50}... | collective-permute-start | bytes 1572872 | tf_op jit(solution)/shard_map/ppermute | solution.py:117
  88.8 19.0 %copy-start.4 = (bf16[8,16,2048]{2,1,0:T(8,128)(2,1)}, bf16[8,16,2048]{2,1,0:T(8,128)(2,1)S(1)}, u32[]{:S(2)}) copy-start(bf16[8,16,2048]{2,1,0:T(8,128)(2,1)S(1)} %collective-permute-done.11.refs_12_) | copy-start | bytes 1572868
  88.8 25.7 %collective-permute-start.8 = (bf16[8,16,2048]{2,1,0:T(8,128)(2,1)S(1)}, bf16[8,16,2048]{2,1,0:T(8,128)(2,1)}, u32[]{:S(2)}, u32[]{:S(2)}) collective-permute-start(bf16[8,16,2048]{2,1,0:T(8,128)(2,1)S(1)} %collective-permute-done.refs_1_), channel_id=1, source_target_pairs={{0,8},{8,0},{1,9},{9,1},{2,10},{10,2},{3,11},{11,3},{4,12},{12,4},... | collective-permute-start | bytes 1572872 | tf_op jit(solution)/shard_map/ppermute | solution.py:117
  93.1 14.9 %copy-start.5 = (bf16[8,16,2048]{2,1,0:T(8,128)(2,1)}, bf16[8,16,2048]{2,1,0:T(8,128)(2,1)S(1)}, u32[]{:S(2)}) copy-start(bf16[8,16,2048]{2,1,0:T(8,128)(2,1)S(1)} %collective-permute-done.9.refs_10_) | copy-start | bytes 1572868
  93.1 21.4 %collective-permute-start.12 = (bf16[8,16,2048]{2,1,0:T(8,128)(2,1)S(1)}, bf16[8,16,2048]{2,1,0:T(8,128)(2,1)}, u32[]{:S(2)}, u32[]{:S(2)}) collective-permute-start(bf16[8,16,2048]{2,1,0:T(8,128)(2,1)S(1)} %collective-permute-done.4.refs_5_), channel_id=1, source_target_pairs={{0,8},{8,0},{1,9},{9,1},{2,10},{10,2},{3,11},{11,3},{4,12},{12,4},... | collective-permute-start | bytes 1572872 | tf_op jit(solution)/shard_map/ppermute | solution.py:117
  95.3 19.3 %collective-permute-start.13 = (bf16[8,16,2048]{2,1,0:T(8,128)(2,1)}, bf16[8,16,2048]{2,1,0:T(8,128)(2,1)}, u32[]{:S(2)}, u32[]{:S(2)}) collective-permute-start(bf16[8,16,2048]{2,1,0:T(8,128)(2,1)} %collective-permute-done.5.refs_6_), channel_id=1, source_target_pairs={{0,8},{8,0},{1,9},{9,1},{2,10},{10,2},{3,11},{11,3},{4,12},{12,4},... | collective-permute-start | bytes 1572872 | tf_op jit(solution)/shard_map/ppermute | solution.py:117
  106.5 8.0 %collective-permute-start.10 = (bf16[8,16,2048]{2,1,0:T(8,128)(2,1)}, bf16[8,16,2048]{2,1,0:T(8,128)(2,1)}, u32[]{:S(2)}, u32[]{:S(2)}) collective-permute-start(bf16[8,16,2048]{2,1,0:T(8,128)(2,1)} %collective-permute-done.2.refs_3_), channel_id=1, source_target_pairs={{0,8},{8,0},{1,9},{9,1},{2,10},{10,2},{3,11},{11,3},{4,12},{12,4},... | collective-permute-start | bytes 1572872 | tf_op jit(solution)/shard_map/ppermute | solution.py:117
  107.8 6.8 %collective-permute-start.14 = (bf16[8,16,2048]{2,1,0:T(8,128)(2,1)}, bf16[8,16,2048]{2,1,0:T(8,128)(2,1)}, u32[]{:S(2)}, u32[]{:S(2)}) collective-permute-start(bf16[8,16,2048]{2,1,0:T(8,128)(2,1)} %collective-permute-done.6.refs_7_), channel_id=1, source_target_pairs={{0,8},{8,0},{1,9},{9,1},{2,10},{10,2},{3,11},{11,3},{4,12},{12,4},... | collective-permute-start | bytes 1572872 | tf_op jit(solution)/shard_map/ppermute | solution.py:117
  111.3 0.7 copy-start
Sparse Core Ops, SparseCore 0:
  30.4 66.2 all-gather.2

commit v2 on v1

v2 whole, which is shorter than its diff:
```python
import jax
import jax.numpy as jnp
from jax import lax
from jax.experimental import pallas as pl
from jax.experimental.pallas import tpu as pltpu
from jax.sharding import Mesh, PartitionSpec as P

ALL = ("xh", "z", "c", "xl", "y")
SIZES = (2, 4, 2, 2, 4)
ROWS = 1000
COLUMNS = 2000
GROUP = 8
OWN = 16
PAIRS = GROUP * GROUP * 2 * OWN
BLOCK = GROUP * 2 * OWN
PADDED = 2048
PANEL = 256
PANELS = PADDED // PANEL
HALF = 1024


def device(xh, z, c, xl, y):
    return (((xh % 2 * 4 + z % 4) * 2 + c) * 2 + xl % 2) * 4 + y % 4


def every():
    return [(xh, z, c, xl, y) for xh in range(2) for z in range(4) for c in range(2) for xl in range(2) for y in range(4)]


def move(value, to):
    return lax.ppermute(value, ALL, [(device(*d), device(*to(*d))) for d in every()])


def swap_cores(value):
    return move(value, lambda xh, z, c, xl, y: (xh, z, 1 - c, xl, y))


def swap_x(value):
    return move(value, lambda xh, z, c, xl, y: (xh, z, c, xl + 1, y) if c == 0 else (xh + 1, z, c, xl, y))


def ring(value, by):
    return move(value, lambda xh, z, c, xl, y: (xh, z, c, xl, y + by) if c == 0 else (xh, z + by, c, xl, y))


def spread(table):
    rows = -(-table.shape[0] // 1024) * 8
    return jnp.pad(table, (0, rows * 128 - table.shape[0])).reshape(rows, 128)


def weights_kernel(valence_ref, conduction_ref, val_ref, cond_ref, omegas_ref, out_ref):
    def lookup(index, table):
        high, low = index // 128, index % 128
        block = lax.broadcasted_iota(jnp.int32, (table.shape[0], PAIRS), 0)
        picked = lax.dot_general(
            table,
            (block == high).astype(jnp.float32),
            (((0,), (0,)), ((), ())),
            precision=lax.Precision.HIGHEST,
            preferred_element_type=jnp.float32,
        )
        lane = lax.broadcasted_iota(jnp.int32, (128, PAIRS), 0)
        return jnp.sum(jnp.where(lane == low, picked, 0.0), axis=0, keepdims=True)

    gap = lookup(conduction_ref[...], cond_ref[...]) - lookup(valence_ref[...], val_ref[...])
    for f in range(2):
        omega = omegas_ref[f]
        out_ref[f : f + 1, :] = -4.0 * gap / (gap * gap + omega * omega)


VMEM = pl.BlockSpec(memory_space=pltpu.VMEM)
SMEM = pl.BlockSpec(memory_space=pltpu.SMEM)


def pair_weights(valence_index, conduction_index, val_energy, cond_energy, omegas):
    def order(index):
        return index.reshape(GROUP, 2, GROUP, OWN).transpose(2, 0, 1, 3).reshape(1, PAIRS)

    return pl.pallas_call(
        weights_kernel,
        out_shape=jax.ShapeDtypeStruct((2, PAIRS), jnp.float32),
        in_specs=[VMEM] * 4 + [SMEM],
        out_specs=VMEM,
        compiler_params=pltpu.CompilerParams(vmem_limit_bytes=24 << 20),
        name="weights",
    )(order(valence_index), order(conduction_index), spread(val_energy), spread(cond_energy), omegas)


def slices_kernel(core_ref, own_ref, other_ref, out_ref):
    core = core_ref[0]
    for s in range(GROUP):
        lanes = slice(s * COLUMNS, (s + 1) * COLUMNS)
        out_ref[s, core, :, :COLUMNS] = own_ref[:, lanes]
        out_ref[s, 1 - core, :, :COLUMNS] = other_ref[:, lanes]
    out_ref[:, :, :, COLUMNS:] = jnp.zeros((GROUP, 2, OWN, PADDED - COLUMNS), jnp.bfloat16)


def slices(core, own, other):
    return pl.pallas_call(
        slices_kernel,
        out_shape=jax.ShapeDtypeStruct((GROUP, 2, OWN, PADDED), jnp.bfloat16),
        in_specs=[SMEM, VMEM, VMEM],
        out_specs=VMEM,
        compiler_params=pltpu.CompilerParams(vmem_limit_bytes=16 << 20),
        name="slices",
    )(core, own, other)


def turn_kernel(core_ref, in_ref, out_ref):
    @pl.when(core_ref[0] == 0)
    def _():
        for half in range(2):
            part = in_ref[:, half * ROWS : (half + 1) * ROWS]
            part = jnp.concatenate([part, jnp.zeros((BLOCK, HALF - ROWS), jnp.bfloat16)], axis=1)
            out_ref[half * HALF : (half + 1) * HALF, :] = part.T

    @pl.when(core_ref[0] == 1)
    def _():
        for p in range(PANELS):
            out_ref[p * BLOCK : (p + 1) * BLOCK, :] = in_ref[:, p * PANEL : (p + 1) * PANEL]


def turn(core, value):
    return pl.pallas_call(
        turn_kernel,
        out_shape=jax.ShapeDtypeStruct((PADDED, BLOCK), jnp.bfloat16),
        in_specs=[SMEM, VMEM],
        out_specs=VMEM,
        compiler_params=pltpu.CompilerParams(vmem_limit_bytes=16 << 20),
        name="turn",
    )(core, value)


def product_kernel(place_ref, weight_ref, *refs):
    mine, theirs = refs[:GROUP], refs[GROUP : 2 * GROUP]
    out_ref, rows, scaled, columns, rows_sem, columns_sem = refs[2 * GROUP :]
    j = pl.program_id(0)
    core = place_ref[0]

    def row_copy(k, refs):
        half = refs[k].at[pl.ds(pl.multiple_of(core * HALF, HALF), HALF)]
        return pltpu.make_async_copy(half, rows.at[place_ref[1 + k]], rows_sem.at[k])

    def column_copy(k, refs):
        block = refs[k].reshape(PANELS, GROUP, 2 * OWN, PANEL)
        return pltpu.make_async_copy(block, columns.at[:, :, place_ref[1 + GROUP + k]], columns_sem.at[k])

    @pl.when(j == 0)
    def _():
        for which, first, second in ((0, mine, theirs), (1, theirs, mine)):

            @pl.when(core == which)
            def _(first=first, second=second):
                for k in range(GROUP):
                    row_copy(k, first).start()
                for k in range(GROUP):
                    column_copy(k, second).start()

        for k in range(GROUP):
            row_copy(k, mine).wait()
        for n in range(GROUP):
            part = rows[n, :ROWS].astype(jnp.float32)
            lanes = slice(n * BLOCK, (n + 1) * BLOCK)
            for f in range(2):
                scaled[f, :, lanes] = (part * weight_ref[f : f + 1, lanes]).astype(jnp.bfloat16)
        for k in range(GROUP):
            column_copy(k, mine).wait()

    right = columns[j].reshape(PAIRS, PANEL)
    for f in range(2):
        out_ref[f] = jnp.dot(scaled[f], right, preferred_element_type=jnp.float32)


def product(place, weight, mine, theirs):
    any_space = pl.BlockSpec(memory_space=pl.ANY)
    return pl.pallas_call(
        product_kernel,
        grid=(PANELS,),
        out_shape=jax.ShapeDtypeStruct((2, ROWS, COLUMNS), jnp.float32),
        in_specs=[SMEM, VMEM] + [any_space] * (2 * GROUP),
        out_specs=pl.BlockSpec((2, ROWS, PANEL), lambda j: (0, 0, j)),
        scratch_shapes=[
            pltpu.VMEM((GROUP, HALF, BLOCK), jnp.bfloat16),
            pltpu.VMEM((2, ROWS, PAIRS), jnp.bfloat16),
            pltpu.VMEM((PANELS, GROUP, GROUP, 2 * OWN, PANEL), jnp.bfloat16),
            pltpu.SemaphoreType.DMA((GROUP,)),
            pltpu.SemaphoreType.DMA((GROUP,)),
        ],
        compiler_params=pltpu.CompilerParams(vmem_limit_bytes=40 << 20),
        cost_estimate=pl.CostEstimate(
            flops=4 * ROWS * COLUMNS * PAIRS, bytes_accessed=28 << 20, transcendentals=0
        ),
        name="product",
    )(place, weight, *mine, *theirs)


def exchange(value):
    wide = [[device(a // 4, a % 4, 0, xl, y) for a in range(GROUP)] for xl in range(2) for y in range(4)]
    narrow = [[device(xh, z, 1, b // 4, b % 4) for b in range(GROUP)] for xh in range(2) for z in range(4)]
    return lax.all_to_all(value, ALL, 0, 0, axis_index_groups=wide + narrow, tiled=True)


def gather(own):
    beside = swap_x(own)
    near = [own, beside]
    up = [ring(v, 1) for v in near]
    down = [ring(v, -1) for v in near]
    far = [ring(up[0], 1), ring(down[1], -1)]
    return near + up + down + far


def places(core):
    def of(x, around):
        shifts = (0, 0, 3, 3, 1, 1, 2, 2)
        return [(x + k) % 2 * 4 + (around + shift) % 4 for k, shift in enumerate(shifts)]

    rows = of(lax.axis_index("xl"), lax.axis_index("y"))
    columns = of(lax.axis_index("xh"), lax.axis_index("z"))
    return jnp.stack([core] + rows + columns).astype(jnp.int32)


def body(pair_elements, valence_index, conduction_index, val_energy, cond_energy, omegas):
    core = lax.axis_index("c").astype(jnp.int32)
    weight = pair_weights(valence_index, conduction_index, val_energy, cond_energy, omegas)
    part = exchange(slices(core[None], pair_elements, swap_cores(pair_elements)))
    mine = gather(turn(core[None], part.reshape(BLOCK, PADDED)))
    theirs = [swap_cores(v) for v in mine]
    return product(places(core), weight, mine, theirs)


def solution(mesh):
    fine = Mesh(mesh.devices.reshape(SIZES), ALL)
    wide, narrow = ("xh", "z", "c"), ("xl", "y")
    return jax.shard_map(
        body,
        mesh=fine,
        in_specs=(P(wide + narrow, None), P(), P(), P(), P(), P()),
        out_specs=P(None, wide, narrow),
        check_vma=False,
    )
```

time: 147 us -> 115 us (0.78)
  blocking collectives: 38.7 us -> 18.1 us
  between operations: 13.6 us -> 0.14 us
  waiting for transfers between devices: 34.4 us -> 29.8 us
  local copies, waits for them, and re-layouts: 9.59 us -> 14 us
  starting transfers between devices: 22.7 us -> 26.1 us
    all_to_all x2 -> x1, blocking collectives: 38.7 us -> 18.1 us  [exchange(): lax.all_to_all(value, ALL, 0, 0, axis_index_groups=wide + narrow, tiled=T...]
    unnamed x12 -> x20, local copies, waits for them, and re-layouts: 0.67 us -> 10.5 us
    ppermute x15 -> x16, waiting for transfers between devices: 34.4 us -> 29.8 us  [move(): lax.ppermute(value, ALL, [(device(*d), device(*to(*d))) for d in every()])]
    ppermute x15 -> x16, starting transfers between devices: 22.7 us -> 26.1 us  [move(): lax.ppermute(value, ALL, [(device(*d), device(*to(*d))) for d in every()])]
    all_to_all x2 -> x0, local copies, waits for them, and re-layouts: 2.3 us -> none  [body(): lax.all_to_all(pair_elements, ('xh', 'z', 'c'), split_axis=1, concat_axis...]
    reshape x6 -> x4, local copies, waits for them, and re-layouts: 3.97 us -> 1.81 us  [order(): index.reshape(GROUP, 2, GROUP, OWN).transpose(2, 0, 1, 3).reshape(1, PAIRS)]
    pallas_call x1 -> x3, Pallas kernels: 24.7 us -> 24.2 us  [the longest x1 23.8 us: product(): pl.pallas_call(product_kernel, grid=(PANELS,), out_shape=jax.ShapeDtypeSt...]
  transfers between devices with their start and end apart: 16 -> 16, of which waited for: 4 -> 4; matrix products, arithmetic and copies ran while one was open for 4% -> 3% of each run, Pallas kernels for 2% -> 2%
where the time goes in v2:
time: 115 us
  waiting for transfers between devices  29.8 us (26%)
  Pallas kernels  26.6 us (23%)
  starting transfers between devices  26.1 us (23%)
  blocking collectives  18.1 us (16%)
  local copies, waits for them, and re-layouts  14 us (12%)
    ppermute x16, waiting for transfers between devices, move(): lax.ppermute(value, ALL, [(device(*d), device(*to(*d))) for d in every()])  29.8 us
    ppermute x16, starting transfers between devices, move(): lax.ppermute(value, ALL, [(device(*d), device(*to(*d))) for d in every()])  26.1 us
    pallas_call x1, Pallas kernels, product(): pl.pallas_call(product_kernel, grid=(PANELS,), out_shape=jax.ShapeDtypeSt...  23.8 us
    all_to_all x1, blocking collectives, exchange(): lax.all_to_all(value, ALL, 0, 0, axis_index_groups=wide + narrow, tiled=T...  18.1 us
    unnamed x20, local copies, waits for them, and re-layouts  10.5 us
    pallas_call x1, Pallas kernels, pair_weights(): pl.pallas_call(weights_kernel, out_shape=jax.ShapeDtypeStruct((2, PAIRS),...  2.42 us
  transfers between devices with their start and end apart: 16, of which 4 were waited for; matrix products, arithmetic and copies ran while one was open for 3% of the time, Pallas kernels for 2%

profile of v2, /device:TPU:1, one launch (start us, length us, event | category | flops | bytes accessed | tf_op | source)
XLA Modules:
  0.0 114.8 jit_solution(10019501228780739971)
XLA Ops:
  0.0 1.4 %collective-permute-start = (bf16[16,16000]{1,0:T(8,128)(2,1)}, bf16[16,16000]{1,0:T(8,128)(2,1)S(1)}, u32[]{:S(2)}, u32[]{:S(2)}) collective-permute-start(bf16[16,16000]{1,0:T(8,128)(2,1)} %own_ref.1), channel_id=1, source_target_pairs={{0,8},{1,9},{2,10},{3,11},{4,12},{5,13},{6,14},{7,15},{8,0},{9,1},... | collective-permute-start | bytes 1536008 | tf_op jit(solution)/shard_map/ppermute | solution.py:31
  1.4 1.7 %collective-permute-done.other_ref = bf16[16,16000]{1,0:T(8,128)(2,1)S(1)} collective-permute-done((bf16[16,16000]{1,0:T(8,128)(2,1)}, bf16[16,16000]{1,0:T(8,128)(2,1)S(1)}, u32[]{:S(2)}, u32[]{:S(2)}) %collective-permute-start) | collective-permute-done | bytes 512032 | tf_op jit(solution)/shard_map/ppermute | solution.py:31
  3.2 0.0 copy-start
  3.2 1.0 copy-done
  4.2 0.3 slices.1
  4.5 18.1 %all_to_all.5 = bf16[8,2,16,2048]{3,2,1,0:T(8,128)(2,1)S(1)} all-to-all(bf16[8,2,16,2048]{3,2,1,0:T(8,128)(2,1)S(1)} %slices.1), channel_id=1, replica_groups={{0,16,32,48,64,80,96,112},{1,17,33,49,65,81,97,113},{2,18,34,50,66,82,9..., dimensions={0} | all-to-all | bytes 2097152 | tf_op jit(solution)/shard_map/all_to_all | solution.py:200
  22.6 0.1 turn.1.refs_0_
  22.7 1.1 collective-permute-start.1
  23.8 4.8 %collective-permute-start.4 = (bf16[2048,256]{1,0:T(8,128)(2,1)S(1)}, bf16[2048,256]{1,0:T(8,128)(2,1)S(1)}, u32[]{:S(2)}, u32[]{:S(2)}) collective-permute-start(bf16[2048,256]{1,0:T(8,128)(2,1)S(1)} %turn.1.refs_0_), channel_id=1, source_target_pairs={{0,3},{1,0},{2,1},{3,2},{4,7},{5,4},{6,5},{7,6},{8,56},{9,57},{10,... | collective-permute-start | bytes 3145736 | tf_op jit(solution)/shard_map/ppermute | solution.py:31
  28.7 0.0 collective-permute-start.2
  28.7 3.9 %collective-permute-start.8 = (bf16[2048,256]{1,0:T(8,128)(2,1)S(1)}, bf16[2048,256]{1,0:T(8,128)(2,1)S(1)}, u32[]{:S(2)}, u32[]{:S(2)}) collective-permute-start(bf16[2048,256]{1,0:T(8,128)(2,1)S(1)} %turn.1.refs_0_), channel_id=1, source_target_pairs={{0,8},{1,9},{2,10},{3,11},{4,12},{5,13},{6,14},{7,15},{8,0},{9,1},... | collective-permute-start | bytes 3145736 | tf_op jit(solution)/shard_map/ppermute | solution.py:31
  32.6 10.4 %collective-permute-done.1.refs_1_ = bf16[2048,256]{1,0:T(8,128)(2,1)S(1)} collective-permute-done((bf16[2048,256]{1,0:T(8,128)(2,1)S(1)}, bf16[2048,256]{1,0:T(8,128)(2,1)S(1)}, u32[]{:S(2)}, u32[]{:S(2)}) %collective-permute-start.1) | collective-permute-done | bytes 1048608 | tf_op jit(solution)/shard_map/ppermute | solution.py:31
  43.0 8.5 %collective-permute-start.5 = (bf16[2048,256]{1,0:T(8,128)(2,1)S(1)}, bf16[2048,256]{1,0:T(8,128)(2,1)}, u32[]{:S(2)}, u32[]{:S(2)}) collective-permute-start(bf16[2048,256]{1,0:T(8,128)(2,1)S(1)} %collective-permute-done.1.refs_1_), channel_id=1, source_target_pairs={{0,3},{1,0},{2,1},{3,2},{4,7},{5,4},{6,5},{7,6},{8,56},{9,57},{10,... | collective-permute-start | bytes 3145736 | tf_op jit(solution)/shard_map/ppermute | solution.py:31
  51.5 0.0 collective-permute-done.4.refs_4_
  51.5 0.0 collective-permute-start.12
  51.5 0.0 collective-permute-done.2.refs_2_
  51.5 0.5 collective-permute-start.10
  52.0 0.0 collective-permute-start.6
  52.0 0.0 copy-start.2
  52.0 1.0 copy-done.2
  53.0 0.0 collective-permute-done.8.refs_8_
  53.0 0.0 copy-start.4
  53.0 1.0 copy-done.4
  54.0 0.8 collective-permute-start.3
  54.8 8.4 %collective-permute-done.5.refs_5_ = bf16[2048,256]{1,0:T(8,128)(2,1)} collective-permute-done((bf16[2048,256]{1,0:T(8,128)(2,1)S(1)}, bf16[2048,256]{1,0:T(8,128)(2,1)}, u32[]{:S(2)}, u32[]{:S(2)}) %collective-permute-start.5) | collective-permute-done | bytes 1048608 | tf_op jit(solution)/shard_map/ppermute | solution.py:31
  63.3 3.5 %collective-permute-start.7 = (bf16[2048,256]{1,0:T(8,128)(2,1)}, bf16[2048,256]{1,0:T(8,128)(2,1)}, u32[]{:S(2)}, u32[]{:S(2)}) collective-permute-start(bf16[2048,256]{1,0:T(8,128)(2,1)} %collective-permute-done.5.refs_5_), channel_id=1, source_target_pairs={{0,3},{1,0},{2,1},{3,2},{4,7},{5,4},{6,5},{7,6},{8,56},{9,57},{10,... | collective-permute-start | bytes 3145736 | tf_op jit(solution)/shard_map/ppermute | solution.py:31
  66.8 0.0 collective-permute-done.12.refs_12_
  66.8 0.0 copy-start.6
  66.8 1.0 copy-done.6
  67.8 0.0 collective-permute-start.9
  67.8 0.0 collective-permute-done.10.refs_10_
  67.8 0.0 copy-start.8
  67.8 1.0 copy-done.8
  68.8 0.5 collective-permute-start.13
  69.3 0.0 collective-permute-done.6.refs_6_
  69.3 0.0 collective-permute-start.14
  69.3 9.2 %collective-permute-done.3.refs_3_ = bf16[2048,256]{1,0:T(8,128)(2,1)} collective-permute-done((bf16[2048,256]{1,0:T(8,128)(2,1)S(1)}, bf16[2048,256]{1,0:T(8,128)(2,1)}, u32[]{:S(2)}, u32[]{:S(2)}) %collective-permute-start.3) | collective-permute-done | bytes 1048608 | tf_op jit(solution)/shard_map/ppermute | solution.py:31
  78.5 0.9 collective-permute-start.11
  79.5 0.0 collective-permute-done.7.refs_7_
  79.5 0.0 collective-permute-start.15
  79.5 0.8 reshape.21
  80.3 0.1 reshape.22.valence_ref
  80.4 0.8 reshape.23
  81.3 0.1 reshape.24.conduction_ref
  81.4 0.7 pad_bitcast_fusion.1.val_ref
  82.1 0.8 pad_bitcast_fusion.cond_ref
  82.9 0.0 copy-start.1
  82.9 0.7 copy-done.1
  83.5 2.4 %weights.1.weight_ref = f32[2,2048]{1,0:T(2,128)S(1)} custom-call(s32[1,2048]{1,0:T(1,128)S(1)} %reshape.22.valence_ref, s32[1,2048]{1,0:T(1,128)S(1)} %reshape.24.conduction_ref, f32[24,128]{1,0:T(8,128)S(1)} %pad_bitcast_fusion.1.val_ref, f32[80,128]{1,0:T(8,128)S(1)} %pad_bitcast_fusion.cond_ref, f32[2]{0:T(128)S(1)} %copy-done.1), custom_call_target="tpu_custom_call" | custom-call | tf_op jit(solution)/shard_map/weights/pallas_call | solution.py:79
  86.0 0.1 stack.71.place_ref
  86.1 0.0 collective-permute-done.9.refs_9_
  86.1 0.0 collective-permute-done.14.refs_14_
  86.1 0.0 collective-permute-done.13.refs_13_
  86.1 0.0 collective-permute-done.11.refs_11_
  86.1 0.0 collective-permute-done.15.refs_15_
  86.1 0.0 copy-start.3
  86.1 1.2 %copy-done.3 = bf16[2048,256]{1,0:T(8,128)(2,1)S(1)} copy-done((bf16[2048,256]{1,0:T(8,128)(2,1)S(1)}, bf16[2048,256]{1,0:T(8,128)(2,1)}, u32[]{:S(2)}) %copy-start.3) | copy-done | bytes 1048600
  87.4 0.0 copy-start.5
  87.4 1.2 %copy-done.5 = bf16[2048,256]{1,0:T(8,128)(2,1)S(1)} copy-done((bf16[2048,256]{1,0:T(8,128)(2,1)S(1)}, bf16[2048,256]{1,0:T(8,128)(2,1)}, u32[]{:S(2)}) %copy-start.5) | copy-done | bytes 1048600
  88.6 0.0 copy-start.7
  88.6 1.2 %copy-done.7 = bf16[2048,256]{1,0:T(8,128)(2,1)S(1)} copy-done((bf16[2048,256]{1,0:T(8,128)(2,1)S(1)}, bf16[2048,256]{1,0:T(8,128)(2,1)}, u32[]{:S(2)}) %copy-start.7) | copy-done | bytes 1048600
  89.8 0.0 copy-start.9
  89.8 1.2 %copy-done.9 = bf16[2048,256]{1,0:T(8,128)(2,1)S(1)} copy-done((bf16[2048,256]{1,0:T(8,128)(2,1)S(1)}, bf16[2048,256]{1,0:T(8,128)(2,1)}, u32[]{:S(2)}) %copy-start.9) | copy-done | bytes 1048600
  91.0 23.8 %product.1 = f32[2,1000,2000]{2,1,0:T(8,128)} custom-call(s32[17]{0:T(128)S(1)} %stack.71.place_ref, f32[2,2048]{1,0:T(2,128)S(1)} %weights.1.weight_ref, bf16[2048,256]{1,0:T(8,128)(2,1)S(1)} %turn.1.refs_0_, bf16[2048,256]{1,0:T(8,128)(2,1)S(1)} %collective-permute-done.1.refs_1_, bf16[2048,256]{1,0:T(8,128)(2,1)S(1)} %copy-done.3, ...), custom_call_target="tpu_custom_call" | custom-call | flops 16384000000 | bytes 29360128 | tf_op jit(solution)/shard_map/product/pallas_call | solution.py:176
  (2 shorter events, 0.1 us)
Async XLA Ops:
  0.0 3.2 %collective-permute-start = (bf16[16,16000]{1,0:T(8,128)(2,1)}, bf16[16,16000]{1,0:T(8,128)(2,1)S(1)}, u32[]{:S(2)}, u32[]{:S(2)}) collective-permute-start(bf16[16,16000]{1,0:T(8,128)(2,1)} %own_ref.1), channel_id=1, source_target_pairs={{0,8},{1,9},{2,10},{3,11},{4,12},{5,13},{6,14},{7,15},{8,0},{9,1},... | collective-permute-start | bytes 1536008 | tf_op jit(solution)/shard_map/ppermute | solution.py:31
  3.2 1.0 copy-start
  22.7 20.3 %collective-permute-start.1 = (bf16[2048,256]{1,0:T(8,128)(2,1)S(1)}, bf16[2048,256]{1,0:T(8,128)(2,1)S(1)}, u32[]{:S(2)}, u32[]{:S(2)}) collective-permute-start(bf16[2048,256]{1,0:T(8,128)(2,1)S(1)} %turn.1.refs_0_), channel_id=1, source_target_pairs={{0,4},{1,5},{2,6},{3,7},{4,0},{5,1},{6,2},{7,3},{8,72},{9,73},{10,... | collective-permute-start | bytes 3145736 | tf_op jit(solution)/shard_map/ppermute | solution.py:31
  23.8 27.7 %collective-permute-start.4 = (bf16[2048,256]{1,0:T(8,128)(2,1)S(1)}, bf16[2048,256]{1,0:T(8,128)(2,1)S(1)}, u32[]{:S(2)}, u32[]{:S(2)}) collective-permute-start(bf16[2048,256]{1,0:T(8,128)(2,1)S(1)} %turn.1.refs_0_), channel_id=1, source_target_pairs={{0,3},{1,0},{2,1},{3,2},{4,7},{5,4},{6,5},{7,6},{8,56},{9,57},{10,... | collective-permute-start | bytes 3145736 | tf_op jit(solution)/shard_map/ppermute | solution.py:31
  28.7 22.9 %collective-permute-start.2 = (bf16[2048,256]{1,0:T(8,128)(2,1)S(1)}, bf16[2048,256]{1,0:T(8,128)(2,1)S(1)}, u32[]{:S(2)}, u32[]{:S(2)}) collective-permute-start(bf16[2048,256]{1,0:T(8,128)(2,1)S(1)} %turn.1.refs_0_), channel_id=1, source_target_pairs={{0,1},{1,2},{2,3},{3,0},{4,5},{5,6},{6,7},{7,4},{8,24},{9,25},{10,... | collective-permute-start | bytes 3145736 | tf_op jit(solution)/shard_map/ppermute | solution.py:31
  28.7 24.4 %collective-permute-start.8 = (bf16[2048,256]{1,0:T(8,128)(2,1)S(1)}, bf16[2048,256]{1,0:T(8,128)(2,1)S(1)}, u32[]{:S(2)}, u32[]{:S(2)}) collective-permute-start(bf16[2048,256]{1,0:T(8,128)(2,1)S(1)} %turn.1.refs_0_), channel_id=1, source_target_pairs={{0,8},{1,9},{2,10},{3,11},{4,12},{5,13},{6,14},{7,15},{8,0},{9,1},... | collective-permute-start | bytes 3145736 | tf_op jit(solution)/shard_map/ppermute | solution.py:31
  43.0 20.2 %collective-permute-start.5 = (bf16[2048,256]{1,0:T(8,128)(2,1)S(1)}, bf16[2048,256]{1,0:T(8,128)(2,1)}, u32[]{:S(2)}, u32[]{:S(2)}) collective-permute-start(bf16[2048,256]{1,0:T(8,128)(2,1)S(1)} %collective-permute-done.1.refs_1_), channel_id=1, source_target_pairs={{0,3},{1,0},{2,1},{3,2},{4,7},{5,4},{6,5},{7,6},{8,56},{9,57},{10,... | collective-permute-start | bytes 3145736 | tf_op jit(solution)/shard_map/ppermute | solution.py:31
  51.5 15.3 %collective-permute-start.12 = (bf16[2048,256]{1,0:T(8,128)(2,1)S(1)}, bf16[2048,256]{1,0:T(8,128)(2,1)S(1)}, u32[]{:S(2)}, u32[]{:S(2)}) collective-permute-start(bf16[2048,256]{1,0:T(8,128)(2,1)S(1)} %collective-permute-done.4.refs_4_), channel_id=1, source_target_pairs={{0,8},{1,9},{2,10},{3,11},{4,12},{5,13},{6,14},{7,15},{8,0},{9,1},... | collective-permute-start | bytes 3145736 | tf_op jit(solution)/shard_map/ppermute | solution.py:31
  51.5 16.2 %collective-permute-start.10 = (bf16[2048,256]{1,0:T(8,128)(2,1)S(1)}, bf16[2048,256]{1,0:T(8,128)(2,1)S(1)}, u32[]{:S(2)}, u32[]{:S(2)}) collective-permute-start(bf16[2048,256]{1,0:T(8,128)(2,1)S(1)} %collective-permute-done.2.refs_2_), channel_id=1, source_target_pairs={{0,8},{1,9},{2,10},{3,11},{4,12},{5,13},{6,14},{7,15},{8,0},{9,1},... | collective-permute-start | bytes 3145736 | tf_op jit(solution)/shard_map/ppermute | solution.py:31
  52.0 17.3 %collective-permute-start.6 = (bf16[2048,256]{1,0:T(8,128)(2,1)S(1)}, bf16[2048,256]{1,0:T(8,128)(2,1)}, u32[]{:S(2)}, u32[]{:S(2)}) collective-permute-start(bf16[2048,256]{1,0:T(8,128)(2,1)S(1)} %collective-permute-done.2.refs_2_), channel_id=1, source_target_pairs={{0,1},{1,2},{2,3},{3,0},{4,5},{5,6},{6,7},{7,4},{8,24},{9,25},{10,... | collective-permute-start | bytes 3145736 | tf_op jit(solution)/shard_map/ppermute | solution.py:31
  52.0 1.0 copy-start.2
  53.0 1.0 copy-start.4
  54.0 24.5 %collective-permute-start.3 = (bf16[2048,256]{1,0:T(8,128)(2,1)S(1)}, bf16[2048,256]{1,0:T(8,128)(2,1)}, u32[]{:S(2)}, u32[]{:S(2)}) collective-permute-start(bf16[2048,256]{1,0:T(8,128)(2,1)S(1)} %collective-permute-done.1.refs_1_), channel_id=1, source_target_pairs={{0,1},{1,2},{2,3},{3,0},{4,5},{5,6},{6,7},{7,4},{8,24},{9,25},{10,... | collective-permute-start | bytes 3145736 | tf_op jit(solution)/shard_map/ppermute | solution.py:31
  63.3 16.2 %collective-permute-start.7 = (bf16[2048,256]{1,0:T(8,128)(2,1)}, bf16[2048,256]{1,0:T(8,128)(2,1)}, u32[]{:S(2)}, u32[]{:S(2)}) collective-permute-start(bf16[2048,256]{1,0:T(8,128)(2,1)} %collective-permute-done.5.refs_5_), channel_id=1, source_target_pairs={{0,3},{1,0},{2,1},{3,2},{4,7},{5,4},{6,5},{7,6},{8,56},{9,57},{10,... | collective-permute-start | bytes 3145736 | tf_op jit(solution)/shard_map/ppermute | solution.py:31
  66.8 1.0 copy-start.6
  67.8 18.3 %collective-permute-start.9 = (bf16[2048,256]{1,0:T(8,128)(2,1)S(1)}, bf16[2048,256]{1,0:T(8,128)(2,1)}, u32[]{:S(2)}, u32[]{:S(2)}) collective-permute-start(bf16[2048,256]{1,0:T(8,128)(2,1)S(1)} %collective-permute-done.1.refs_1_), channel_id=1, source_target_pairs={{0,8},{1,9},{2,10},{3,11},{4,12},{5,13},{6,14},{7,15},{8,0},{9,1},... | collective-permute-start | bytes 3145736 | tf_op jit(solution)/shard_map/ppermute | solution.py:31
  67.8 1.0 copy-start.8
  68.8 17.3 %collective-permute-start.13 = (bf16[2048,256]{1,0:T(8,128)(2,1)}, bf16[2048,256]{1,0:T(8,128)(2,1)}, u32[]{:S(2)}, u32[]{:S(2)}) collective-permute-start(bf16[2048,256]{1,0:T(8,128)(2,1)} %collective-permute-done.5.refs_5_), channel_id=1, source_target_pairs={{0,8},{1,9},{2,10},{3,11},{4,12},{5,13},{6,14},{7,15},{8,0},{9,1},... | collective-permute-start | bytes 3145736 | tf_op jit(solution)/shard_map/ppermute | solution.py:31
  69.3 16.8 %collective-permute-start.14 = (bf16[2048,256]{1,0:T(8,128)(2,1)}, bf16[2048,256]{1,0:T(8,128)(2,1)}, u32[]{:S(2)}, u32[]{:S(2)}) collective-permute-start(bf16[2048,256]{1,0:T(8,128)(2,1)} %collective-permute-done.6.refs_6_), channel_id=1, source_target_pairs={{0,8},{1,9},{2,10},{3,11},{4,12},{5,13},{6,14},{7,15},{8,0},{9,1},... | collective-permute-start | bytes 3145736 | tf_op jit(solution)/shard_map/ppermute | solution.py:31
  78.5 7.6 %collective-permute-start.11 = (bf16[2048,256]{1,0:T(8,128)(2,1)}, bf16[2048,256]{1,0:T(8,128)(2,1)}, u32[]{:S(2)}, u32[]{:S(2)}) collective-permute-start(bf16[2048,256]{1,0:T(8,128)(2,1)} %collective-permute-done.3.refs_3_), channel_id=1, source_target_pairs={{0,8},{1,9},{2,10},{3,11},{4,12},{5,13},{6,14},{7,15},{8,0},{9,1},... | collective-permute-start | bytes 3145736 | tf_op jit(solution)/shard_map/ppermute | solution.py:31
  79.5 6.7 %collective-permute-start.15 = (bf16[2048,256]{1,0:T(8,128)(2,1)}, bf16[2048,256]{1,0:T(8,128)(2,1)}, u32[]{:S(2)}, u32[]{:S(2)}) collective-permute-start(bf16[2048,256]{1,0:T(8,128)(2,1)} %collective-permute-done.7.refs_7_), channel_id=1, source_target_pairs={{0,8},{1,9},{2,10},{3,11},{4,12},{5,13},{6,14},{7,15},{8,0},{9,1},... | collective-permute-start | bytes 3145736 | tf_op jit(solution)/shard_map/ppermute | solution.py:31
  82.9 0.7 copy-start.1
  86.1 1.2 %copy-start.3 = (bf16[2048,256]{1,0:T(8,128)(2,1)S(1)}, bf16[2048,256]{1,0:T(8,128)(2,1)}, u32[]{:S(2)}) copy-start(bf16[2048,256]{1,0:T(8,128)(2,1)} %copy-done.2) | copy-start | bytes 3145732
  87.4 1.2 %copy-start.5 = (bf16[2048,256]{1,0:T(8,128)(2,1)S(1)}, bf16[2048,256]{1,0:T(8,128)(2,1)}, u32[]{:S(2)}) copy-start(bf16[2048,256]{1,0:T(8,128)(2,1)} %copy-done.4) | copy-start | bytes 3145732
  88.6 1.2 %copy-start.7 = (bf16[2048,256]{1,0:T(8,128)(2,1)S(1)}, bf16[2048,256]{1,0:T(8,128)(2,1)}, u32[]{:S(2)}) copy-start(bf16[2048,256]{1,0:T(8,128)(2,1)} %copy-done.6) | copy-start | bytes 3145732
  89.8 1.2 %copy-start.9 = (bf16[2048,256]{1,0:T(8,128)(2,1)S(1)}, bf16[2048,256]{1,0:T(8,128)(2,1)}, u32[]{:S(2)}) copy-start(bf16[2048,256]{1,0:T(8,128)(2,1)} %copy-done.8) | copy-start | bytes 3145732

commit v3 on v2

--- a/solution.py
+++ b/solution.py
@@ -17,6 +17,8 @@
 PANEL = 256
 PANELS = PADDED // PANEL
 HALF = 1024
+WIDTH = 2
+STEPS = PANELS // WIDTH
 
 
 def device(xh, z, c, xl, y):
@@ -131,62 +133,88 @@
     )(core, value)
 
 
+RING = (0, 3, 1, 2)
+
+
+def half_of(refs, k, which):
+    if k == GROUP - 1:
+        return refs[k + which]
+    return refs[k].at[pl.ds(which * HALF, HALF)]
+
+
 def product_kernel(place_ref, weight_ref, *refs):
-    mine, theirs = refs[:GROUP], refs[GROUP : 2 * GROUP]
-    out_ref, rows, scaled, columns, rows_sem, columns_sem = refs[2 * GROUP :]
+    mine, theirs = refs[: GROUP + 1], refs[GROUP + 1 : 2 * GROUP + 2]
+    out_ref, rows, scaled, columns, rows_sem, columns_sem = refs[2 * GROUP + 2 :]
     j = pl.program_id(0)
     core = place_ref[0]
 
-    def row_copy(k, refs):
-        half = refs[k].at[pl.ds(pl.multiple_of(core * HALF, HALF), HALF)]
-        return pltpu.make_async_copy(half, rows.at[place_ref[1 + k]], rows_sem.at[k])
-
-    def column_copy(k, refs):
-        block = refs[k].reshape(PANELS, GROUP, 2 * OWN, PANEL)
-        return pltpu.make_async_copy(block, columns.at[:, :, place_ref[1 + GROUP + k]], columns_sem.at[k])
+    def row_copy(k, which, refs):
+        return pltpu.make_async_copy(half_of(refs, k, which), rows.at[place_ref[1 + k]], rows_sem.at[k])
+
+    def column_copy(k, step, refs):
+        which, part = divmod(step, STEPS // 2)
+        half = half_of(refs, k, which).at[pl.ds(part * WIDTH * BLOCK, WIDTH * BLOCK)]
+        to = columns.at[pl.ds(step * WIDTH, WIDTH), :, place_ref[1 + GROUP + k]]
+        return pltpu.make_async_copy(half.reshape(WIDTH, GROUP, 2 * OWN, PANEL), to, columns_sem.at[step, k])
 
     @pl.when(j == 0)
     def _():
         for which, first, second in ((0, mine, theirs), (1, theirs, mine)):
 
             @pl.when(core == which)
-            def _(first=first, second=second):
+            def _(which=which, first=first, second=second):
                 for k in range(GROUP):
-                    row_copy(k, first).start()
+                    row_copy(k, which, first).start()
                 for k in range(GROUP):
-                    column_copy(k, second).start()
+                    column_copy(k, 0, second).start()
 
         for k in range(GROUP):
-            row_copy(k, mine).wait()
+            row_copy(k, 0, mine).wait()
+
+        for which, second in ((0, theirs), (1, mine)):
+
+            @pl.when(core == which)
+            def _(second=second):
+                for step in range(1, STEPS):
+                    for k in range(GROUP):
+                        column_copy(k, step, second).start()
+
         for n in range(GROUP):
             part = rows[n, :ROWS].astype(jnp.float32)
             lanes = slice(n * BLOCK, (n + 1) * BLOCK)
             for f in range(2):
                 scaled[f, :, lanes] = (part * weight_ref[f : f + 1, lanes]).astype(jnp.bfloat16)
-        for k in range(GROUP):
-            column_copy(k, mine).wait()
-
-    right = columns[j].reshape(PAIRS, PANEL)
-    for f in range(2):
-        out_ref[f] = jnp.dot(scaled[f], right, preferred_element_type=jnp.float32)
+
+    for step in range(STEPS):
+
+        @pl.when(j == step)
+        def _(step=step):
+            for k in range(GROUP):
+                column_copy(k, step, mine).wait()
+
+    for panel in range(WIDTH):
+        right = columns[j * WIDTH + panel].reshape(PAIRS, PANEL)
+        for f in range(2):
+            out_ref[f, :, panel * PANEL : (panel + 1) * PANEL] = jnp.dot(
+                scaled[f], right, preferred_element_type=jnp.float32
+            )
 
 
 def product(place, weight, mine, theirs):
-    any_space = pl.BlockSpec(memory_space=pl.ANY)
     return pl.pallas_call(
         product_kernel,
-        grid=(PANELS,),
+        grid=(STEPS,),
         out_shape=jax.ShapeDtypeStruct((2, ROWS, COLUMNS), jnp.float32),
-        in_specs=[SMEM, VMEM] + [any_space] * (2 * GROUP),
-        out_specs=pl.BlockSpec((2, ROWS, PANEL), lambda j: (0, 0, j)),
+        in_specs=[SMEM, VMEM] + [pl.BlockSpec(memory_space=pl.ANY)] * (2 * GROUP + 2),
+        out_specs=pl.BlockSpec((2, ROWS, WIDTH * PANEL), lambda j: (0, 0, j)),
         scratch_shapes=[
             pltpu.VMEM((GROUP, HALF, BLOCK), jnp.bfloat16),
             pltpu.VMEM((2, ROWS, PAIRS), jnp.bfloat16),
             pltpu.VMEM((PANELS, GROUP, GROUP, 2 * OWN, PANEL), jnp.bfloat16),
             pltpu.SemaphoreType.DMA((GROUP,)),
-            pltpu.SemaphoreType.DMA((GROUP,)),
+            pltpu.SemaphoreType.DMA((STEPS, GROUP)),
         ],
-        compiler_params=pltpu.CompilerParams(vmem_limit_bytes=40 << 20),
+        compiler_params=pltpu.CompilerParams(vmem_limit_bytes=32 << 20),
         cost_estimate=pl.CostEstimate(
             flops=4 * ROWS * COLUMNS * PAIRS, bytes_accessed=28 << 20, transcendentals=0
         ),
@@ -200,19 +228,19 @@
     return lax.all_to_all(value, ALL, 0, 0, axis_index_groups=wide + narrow, tiled=True)
 
 
-def gather(own):
+def gather(own, weight, place):
+    near = [ring(own, by) for by in (1, -1, 2)]
     beside = swap_x(own)
-    near = [own, beside]
-    up = [ring(v, 1) for v in near]
-    down = [ring(v, -1) for v in near]
-    far = [ring(up[0], 1), ring(down[1], -1)]
-    return near + up + down + far
+    near, beside, weight, place = lax.optimization_barrier((near, beside, weight, place))
+    late = [ring(beside, by) for by in (1, -1)]
+    far = [swap_x(near[2][:HALF]), ring(beside[HALF:], 2)]
+    mine = [own] + near + [beside] + late + far
+    return mine, [swap_cores(v) for v in mine], weight, place
 
 
 def places(core):
     def of(x, around):
-        shifts = (0, 0, 3, 3, 1, 1, 2, 2)
-        return [(x + k) % 2 * 4 + (around + shift) % 4 for k, shift in enumerate(shifts)]
+        return [(x + k) % 2 * 4 + (around + shift) % 4 for k in range(2) for shift in RING]
 
     rows = of(lax.axis_index("xl"), lax.axis_index("y"))
     columns = of(lax.axis_index("xh"), lax.axis_index("z"))
@@ -223,9 +251,8 @@
     core = lax.axis_index("c").astype(jnp.int32)
     weight = pair_weights(valence_index, conduction_index, val_energy, cond_energy, omegas)
     part = exchange(slices(core[None], pair_elements, swap_cores(pair_elements)))
-    mine = gather(turn(core[None], part.reshape(BLOCK, PADDED)))
-    theirs = [swap_cores(v) for v in mine]
-    return product(places(core), weight, mine, theirs)
+    mine, theirs, weight, place = gather(turn(core[None], part.reshape(BLOCK, PADDED)), weight, places(core))
+    return product(place, weight, mine, theirs)
 
 
 def solution(mesh):

time: 115 us -> 108 us (0.939)
  starting transfers between devices: 26.1 us -> 35.2 us
  local copies, waits for them, and re-layouts: 14 us -> 5.25 us
  waiting for transfers between devices: 29.8 us -> 22 us
    ppermute x16 -> x18, starting transfers between devices: 26.1 us -> 35.2 us  [move(): lax.ppermute(value, ALL, [(device(*d), device(*to(*d))) for d in every()])]
    unnamed x20 -> x4, local copies, waits for them, and re-layouts: 10.5 us -> 1.69 us
    ppermute x16 -> x18, waiting for transfers between devices: 29.8 us -> 22 us  [move(): lax.ppermute(value, ALL, [(device(*d), device(*to(*d))) for d in every()])]
  transfers between devices with their start and end apart: 16 -> 18, of which waited for: 4 -> 8; matrix products, arithmetic and copies ran while one was open for 3% -> 3% of each run, Pallas kernels for 2% -> 2%
where the time goes in v3:
time: 108 us; the launch traced here: 107 us
  starting transfers between devices  35.2 us (33%)
  Pallas kernels  26.5 us (25%)
  waiting for transfers between devices  22 us (20%)
  blocking collectives  18.1 us (17%)
  local copies, waits for them, and re-layouts  5.25 us (5%)
    ppermute x18, starting transfers between devices, move(): lax.ppermute(value, ALL, [(device(*d), device(*to(*d))) for d in every()])  35.2 us
    pallas_call x1, Pallas kernels, product(): pl.pallas_call(product_kernel, grid=(STEPS,), out_shape=jax.ShapeDtypeStr...  23.7 us
    ppermute x18, waiting for transfers between devices, move(): lax.ppermute(value, ALL, [(device(*d), device(*to(*d))) for d in every()])  22 us
    all_to_all x1, blocking collectives, exchange(): lax.all_to_all(value, ALL, 0, 0, axis_index_groups=wide + narrow, tiled=T...  18.1 us
    pallas_call x1, Pallas kernels, pair_weights(): pl.pallas_call(weights_kernel, out_shape=jax.ShapeDtypeStruct((2, PAIRS),...  2.42 us
  transfers between devices with their start and end apart: 18, of which 8 were waited for; matrix products, arithmetic and copies ran while one was open for 3% of the time, Pallas kernels for 2%

profile of v3, /device:TPU:1, one launch (start us, length us, event | category | flops | bytes accessed | tf_op | source)
XLA Modules:
  0.0 107.4 jit_solution(8007939783416486459)
XLA Ops:
  0.0 1.4 %collective-permute-start = (bf16[16,16000]{1,0:T(8,128)(2,1)}, bf16[16,16000]{1,0:T(8,128)(2,1)S(1)}, u32[]{:S(2)}, u32[]{:S(2)}) collective-permute-start(bf16[16,16000]{1,0:T(8,128)(2,1)} %own_ref.1), channel_id=1, source_target_pairs={{0,8},{1,9},{2,10},{3,11},{4,12},{5,13},{6,14},{7,15},{8,0},{9,1},... | collective-permute-start | bytes 1536008 | tf_op jit(solution)/shard_map/ppermute | solution.py:33
  1.4 1.7 %collective-permute-done.other_ref = bf16[16,16000]{1,0:T(8,128)(2,1)S(1)} collective-permute-done((bf16[16,16000]{1,0:T(8,128)(2,1)}, bf16[16,16000]{1,0:T(8,128)(2,1)S(1)}, u32[]{:S(2)}, u32[]{:S(2)}) %collective-permute-start) | collective-permute-done | bytes 512032 | tf_op jit(solution)/shard_map/ppermute | solution.py:33
  3.2 0.0 copy-start
  3.2 1.0 copy-done
  4.2 0.3 slices.1
  4.5 18.1 %all_to_all.5 = bf16[8,2,16,2048]{3,2,1,0:T(8,128)(2,1)S(1)} all-to-all(bf16[8,2,16,2048]{3,2,1,0:T(8,128)(2,1)S(1)} %slices.1), channel_id=1, replica_groups={{0,16,32,48,64,80,96,112},{1,17,33,49,65,81,97,113},{2,18,34,50,66,82,9..., dimensions={0} | all-to-all | bytes 2097152 | tf_op jit(solution)/shard_map/all_to_all | solution.py:228
  22.6 0.1 turn.1.refs_0_
  22.7 1.1 %collective-permute-start.4 = (bf16[2048,256]{1,0:T(8,128)(2,1)S(1)}, bf16[2048,256]{1,0:T(8,128)(2,1)S(1)}, u32[]{:S(2)}, u32[]{:S(2)}) collective-permute-start(bf16[2048,256]{1,0:T(8,128)(2,1)S(1)} %turn.1.refs_0_), channel_id=1, source_target_pairs={{0,4},{1,5},{2,6},{3,7},{4,0},{5,1},{6,2},{7,3},{8,72},{9,73},{10,... | collective-permute-start | bytes 3145736 | tf_op jit(solution)/shard_map/ppermute | solution.py:33
  23.8 4.3 %collective-permute-start.3 = (bf16[2048,256]{1,0:T(8,128)(2,1)S(1)}, bf16[2048,256]{1,0:T(8,128)(2,1)S(1)}, u32[]{:S(2)}, u32[]{:S(2)}) collective-permute-start(bf16[2048,256]{1,0:T(8,128)(2,1)S(1)} %turn.1.refs_0_), channel_id=1, source_target_pairs={{0,2},{1,3},{2,0},{3,1},{4,6},{5,7},{6,4},{7,5},{8,40},{9,41},{10,... | collective-permute-start | bytes 3145736 | tf_op jit(solution)/shard_map/ppermute | solution.py:33
  28.1 0.5 collective-permute-start.2
  28.7 0.9 collective-permute-start.1
  29.6 5.4 %collective-permute-start.9 = (bf16[2048,256]{1,0:T(8,128)(2,1)S(1)}, bf16[2048,256]{1,0:T(8,128)(2,1)}, u32[]{:S(2)}, u32[]{:S(2)}) collective-permute-start(bf16[2048,256]{1,0:T(8,128)(2,1)S(1)} %turn.1.refs_0_), channel_id=1, source_target_pairs={{0,8},{1,9},{2,10},{3,11},{4,12},{5,13},{6,14},{7,15},{8,0},{9,1},... | collective-permute-start | bytes 3145736 | tf_op jit(solution)/shard_map/ppermute | solution.py:33
  35.0 0.8 reshape.22
  35.8 0.1 reshape.23.valence_ref
  35.9 0.8 reshape.24
  36.7 0.1 reshape.25.conduction_ref
  36.9 0.7 pad_bitcast_fusion.1.val_ref
  37.6 0.8 pad_bitcast_fusion.cond_ref
  38.4 0.0 copy-start.1
  38.4 0.7 copy-done.1
  39.0 2.4 %weights.1.weight_ref = f32[2,2048]{1,0:T(2,128)S(1)} custom-call(s32[1,2048]{1,0:T(1,128)S(1)} %reshape.23.valence_ref, s32[1,2048]{1,0:T(1,128)S(1)} %reshape.25.conduction_ref, f32[24,128]{1,0:T(8,128)S(1)} %pad_bitcast_fusion.1.val_ref, f32[80,128]{1,0:T(8,128)S(1)} %pad_bitcast_fusion.cond_ref, f32[2]{0:T(128)S(1)} %copy-done.1), custom_call_target="tpu_custom_call" | custom-call | tf_op jit(solution)/shard_map/weights/pallas_call | solution.py:81
  41.5 0.1 stack.68.place_ref
  41.6 1.7 %collective-permute-done.4.refs_4_ = bf16[2048,256]{1,0:T(8,128)(2,1)S(1)} collective-permute-done((bf16[2048,256]{1,0:T(8,128)(2,1)S(1)}, bf16[2048,256]{1,0:T(8,128)(2,1)S(1)}, u32[]{:S(2)}, u32[]{:S(2)}) %collective-permute-start.4) | collective-permute-done | bytes 1048608 | tf_op jit(solution)/shard_map/ppermute | solution.py:33
  43.3 0.0 collective-permute-done.3.refs_3_
  43.3 9.8 %collective-permute-done.2.refs_2_ = bf16[2048,256]{1,0:T(8,128)(2,1)} collective-permute-done((bf16[2048,256]{1,0:T(8,128)(2,1)S(1)}, bf16[2048,256]{1,0:T(8,128)(2,1)}, u32[]{:S(2)}, u32[]{:S(2)}) %collective-permute-start.2) | collective-permute-done | bytes 1048608 | tf_op jit(solution)/shard_map/ppermute | solution.py:33
  53.1 0.0 collective-permute-done.1.refs_1_
  53.1 1.9 %collective-permute-start.8 = (bf16[1024,256]{1,0:T(8,128)(2,1)S(1)}, bf16[1024,256]{1,0:T(8,128)(2,1)S(1)}, u32[]{:S(2)}, u32[]{:S(2)}) collective-permute-start(bf16[1024,256]{1,0:T(8,128)(2,1)S(1)} %slice.7), channel_id=1, source_target_pairs={{0,2},{1,3},{2,0},{3,1},{4,6},{5,7},{6,4},{7,5},{8,40},{9,41},{10,... | collective-permute-start | bytes 1572872 | tf_op jit(solution)/shard_map/ppermute | solution.py:33
  55.1 1.6 %collective-permute-start.7 = (bf16[1024,256]{1,0:T(8,128)(2,1)S(1)}, bf16[1024,256]{1,0:T(8,128)(2,1)S(1)}, u32[]{:S(2)}, u32[]{:S(2)}) collective-permute-start(bf16[1024,256]{1,0:T(8,128)(2,1)S(1)} %slice.6), channel_id=1, source_target_pairs={{0,4},{1,5},{2,6},{3,7},{4,0},{5,1},{6,2},{7,3},{8,72},{9,73},{10,... | collective-permute-start | bytes 1572872 | tf_op jit(solution)/shard_map/ppermute | solution.py:33
  56.7 5.2 %collective-permute-start.10 = (bf16[2048,256]{1,0:T(8,128)(2,1)}, bf16[2048,256]{1,0:T(8,128)(2,1)S(1)}, u32[]{:S(2)}, u32[]{:S(2)}) collective-permute-start(bf16[2048,256]{1,0:T(8,128)(2,1)} %collective-permute-done.1.refs_1_), channel_id=1, source_target_pairs={{0,8},{1,9},{2,10},{3,11},{4,12},{5,13},{6,14},{7,15},{8,0},{9,1},... | collective-permute-start | bytes 3145736 | tf_op jit(solution)/shard_map/ppermute | solution.py:33
  61.9 0.6 collective-permute-start.6
  62.6 0.0 collective-permute-done.9.refs_9_
  62.6 0.8 collective-permute-start.5
  63.4 0.0 collective-permute-done.8.refs_8_
  63.4 5.1 %collective-permute-start.17 = (bf16[1024,256]{1,0:T(8,128)(2,1)S(1)}, bf16[1024,256]{1,0:T(8,128)(2,1)S(1)}, u32[]{:S(2)}, u32[]{:S(2)}) collective-permute-start(bf16[1024,256]{1,0:T(8,128)(2,1)S(1)} %collective-permute-done.8.refs_8_), channel_id=1, source_target_pairs={{0,8},{1,9},{2,10},{3,11},{4,12},{5,13},{6,14},{7,15},{8,0},{9,1},... | collective-permute-start | bytes 1572872 | tf_op jit(solution)/shard_map/ppermute | solution.py:33
  68.5 0.0 collective-permute-done.7.refs_7_
  68.5 1.5 %collective-permute-start.16 = (bf16[1024,256]{1,0:T(8,128)(2,1)S(1)}, bf16[1024,256]{1,0:T(8,128)(2,1)S(1)}, u32[]{:S(2)}, u32[]{:S(2)}) collective-permute-start(bf16[1024,256]{1,0:T(8,128)(2,1)S(1)} %collective-permute-done.7.refs_7_), channel_id=1, source_target_pairs={{0,8},{1,9},{2,10},{3,11},{4,12},{5,13},{6,14},{7,15},{8,0},{9,1},... | collective-permute-start | bytes 1572872 | tf_op jit(solution)/shard_map/ppermute | solution.py:33
  70.0 0.1 collective-permute-done.17.refs_17_
  70.1 0.4 collective-permute-start.12
  70.4 1.1 %collective-permute-done.16.refs_16_ = bf16[1024,256]{1,0:T(8,128)(2,1)S(1)} collective-permute-done((bf16[1024,256]{1,0:T(8,128)(2,1)S(1)}, bf16[1024,256]{1,0:T(8,128)(2,1)S(1)}, u32[]{:S(2)}, u32[]{:S(2)}) %collective-permute-start.16) | collective-permute-done | bytes 524320 | tf_op jit(solution)/shard_map/ppermute | solution.py:33
  71.5 0.4 collective-permute-start.13
  71.9 0.0 collective-permute-done.10.refs_10_
  71.9 0.1 collective-permute-start.11
  72.0 3.8 %collective-permute-done.6.refs_6_ = bf16[2048,256]{1,0:T(8,128)(2,1)S(1)} collective-permute-done((bf16[2048,256]{1,0:T(8,128)(2,1)S(1)}, bf16[2048,256]{1,0:T(8,128)(2,1)S(1)}, u32[]{:S(2)}, u32[]{:S(2)}) %collective-permute-start.6) | collective-permute-done | bytes 1048608 | tf_op jit(solution)/shard_map/ppermute | solution.py:33
  75.9 3.8 %collective-permute-start.15 = (bf16[2048,256]{1,0:T(8,128)(2,1)S(1)}, bf16[2048,256]{1,0:T(8,128)(2,1)S(1)}, u32[]{:S(2)}, u32[]{:S(2)}) collective-permute-start(bf16[2048,256]{1,0:T(8,128)(2,1)S(1)} %collective-permute-done.6.refs_6_), channel_id=1, source_target_pairs={{0,8},{1,9},{2,10},{3,11},{4,12},{5,13},{6,14},{7,15},{8,0},{9,1},... | collective-permute-start | bytes 3145736 | tf_op jit(solution)/shard_map/ppermute | solution.py:33
  79.7 0.0 collective-permute-done.5.refs_5_
  79.7 0.0 collective-permute-start.14
  79.7 0.0 collective-permute-done.11.refs_11_
  79.7 0.0 collective-permute-done.12.refs_12_
  79.7 0.0 collective-permute-done.13.refs_13_
  79.7 2.3 %collective-permute-done.15.refs_15_ = bf16[2048,256]{1,0:T(8,128)(2,1)S(1)} collective-permute-done((bf16[2048,256]{1,0:T(8,128)(2,1)S(1)}, bf16[2048,256]{1,0:T(8,128)(2,1)S(1)}, u32[]{:S(2)}, u32[]{:S(2)}) %collective-permute-start.15) | collective-permute-done | bytes 1048608 | tf_op jit(solution)/shard_map/ppermute | solution.py:33
  82.0 1.5 %collective-permute-done.14.refs_14_ = bf16[2048,256]{1,0:T(8,128)(2,1)S(1)} collective-permute-done((bf16[2048,256]{1,0:T(8,128)(2,1)S(1)}, bf16[2048,256]{1,0:T(8,128)(2,1)S(1)}, u32[]{:S(2)}, u32[]{:S(2)}) %collective-permute-start.14) | collective-permute-done | bytes 1048608 | tf_op jit(solution)/shard_map/ppermute | solution.py:33
  83.5 23.7 %product.1 = f32[2,1000,2000]{2,1,0:T(8,128)} custom-call(s32[17]{0:T(128)S(1)} %stack.68.place_ref, f32[2,2048]{1,0:T(2,128)S(1)} %weights.1.weight_ref, bf16[2048,256]{1,0:T(8,128)(2,1)S(1)} %turn.1.refs_0_, bf16[2048,256]{1,0:T(8,128)(2,1)} %collective-permute-done.1.refs_1_, bf16[2048,256]{1,0:T(8,128)(2,1)} %collective-permute-done.2.refs_2_, ...), custom_call_target="tpu_custom_call" | custom-call | flops 16384000000 | bytes 29360128 | tf_op jit(solution)/shard_map/product/pallas_call | solution.py:204
  (4 shorter events, 0.1 us)
Async XLA Ops:
  0.0 3.2 %collective-permute-start = (bf16[16,16000]{1,0:T(8,128)(2,1)}, bf16[16,16000]{1,0:T(8,128)(2,1)S(1)}, u32[]{:S(2)}, u32[]{:S(2)}) collective-permute-start(bf16[16,16000]{1,0:T(8,128)(2,1)} %own_ref.1), channel_id=1, source_target_pairs={{0,8},{1,9},{2,10},{3,11},{4,12},{5,13},{6,14},{7,15},{8,0},{9,1},... | collective-permute-start | bytes 1536008 | tf_op jit(solution)/shard_map/ppermute | solution.py:33
  3.2 1.0 copy-start
  22.7 20.6 %collective-permute-start.4 = (bf16[2048,256]{1,0:T(8,128)(2,1)S(1)}, bf16[2048,256]{1,0:T(8,128)(2,1)S(1)}, u32[]{:S(2)}, u32[]{:S(2)}) collective-permute-start(bf16[2048,256]{1,0:T(8,128)(2,1)S(1)} %turn.1.refs_0_), channel_id=1, source_target_pairs={{0,4},{1,5},{2,6},{3,7},{4,0},{5,1},{6,2},{7,3},{8,72},{9,73},{10,... | collective-permute-start | bytes 3145736 | tf_op jit(solution)/shard_map/ppermute | solution.py:33
  23.8 19.5 %collective-permute-start.3 = (bf16[2048,256]{1,0:T(8,128)(2,1)S(1)}, bf16[2048,256]{1,0:T(8,128)(2,1)S(1)}, u32[]{:S(2)}, u32[]{:S(2)}) collective-permute-start(bf16[2048,256]{1,0:T(8,128)(2,1)S(1)} %turn.1.refs_0_), channel_id=1, source_target_pairs={{0,2},{1,3},{2,0},{3,1},{4,6},{5,7},{6,4},{7,5},{8,40},{9,41},{10,... | collective-permute-start | bytes 3145736 | tf_op jit(solution)/shard_map/ppermute | solution.py:33
  28.1 25.0 %collective-permute-start.2 = (bf16[2048,256]{1,0:T(8,128)(2,1)S(1)}, bf16[2048,256]{1,0:T(8,128)(2,1)}, u32[]{:S(2)}, u32[]{:S(2)}) collective-permute-start(bf16[2048,256]{1,0:T(8,128)(2,1)S(1)} %turn.1.refs_0_), channel_id=1, source_target_pairs={{0,3},{1,0},{2,1},{3,2},{4,7},{5,4},{6,5},{7,6},{8,56},{9,57},{10,... | collective-permute-start | bytes 3145736 | tf_op jit(solution)/shard_map/ppermute | solution.py:33
  28.7 24.4 %collective-permute-start.1 = (bf16[2048,256]{1,0:T(8,128)(2,1)S(1)}, bf16[2048,256]{1,0:T(8,128)(2,1)}, u32[]{:S(2)}, u32[]{:S(2)}) collective-permute-start(bf16[2048,256]{1,0:T(8,128)(2,1)S(1)} %turn.1.refs_0_), channel_id=1, source_target_pairs={{0,1},{1,2},{2,3},{3,0},{4,5},{5,6},{6,7},{7,4},{8,24},{9,25},{10,... | collective-permute-start | bytes 3145736 | tf_op jit(solution)/shard_map/ppermute | solution.py:33
  29.6 33.0 %collective-permute-start.9 = (bf16[2048,256]{1,0:T(8,128)(2,1)S(1)}, bf16[2048,256]{1,0:T(8,128)(2,1)}, u32[]{:S(2)}, u32[]{:S(2)}) collective-permute-start(bf16[2048,256]{1,0:T(8,128)(2,1)S(1)} %turn.1.refs_0_), channel_id=1, source_target_pairs={{0,8},{1,9},{2,10},{3,11},{4,12},{5,13},{6,14},{7,15},{8,0},{9,1},... | collective-permute-start | bytes 3145736 | tf_op jit(solution)/shard_map/ppermute | solution.py:33
  38.4 0.7 copy-start.1
  53.1 10.3 %collective-permute-start.8 = (bf16[1024,256]{1,0:T(8,128)(2,1)S(1)}, bf16[1024,256]{1,0:T(8,128)(2,1)S(1)}, u32[]{:S(2)}, u32[]{:S(2)}) collective-permute-start(bf16[1024,256]{1,0:T(8,128)(2,1)S(1)} %slice.7), channel_id=1, source_target_pairs={{0,2},{1,3},{2,0},{3,1},{4,6},{5,7},{6,4},{7,5},{8,40},{9,41},{10,... | collective-permute-start | bytes 1572872 | tf_op jit(solution)/shard_map/ppermute | solution.py:33
  55.1 13.4 %collective-permute-start.7 = (bf16[1024,256]{1,0:T(8,128)(2,1)S(1)}, bf16[1024,256]{1,0:T(8,128)(2,1)S(1)}, u32[]{:S(2)}, u32[]{:S(2)}) collective-permute-start(bf16[1024,256]{1,0:T(8,128)(2,1)S(1)} %slice.6), channel_id=1, source_target_pairs={{0,4},{1,5},{2,6},{3,7},{4,0},{5,1},{6,2},{7,3},{8,72},{9,73},{10,... | collective-permute-start | bytes 1572872 | tf_op jit(solution)/shard_map/ppermute | solution.py:33
  56.7 15.2 %collective-permute-start.10 = (bf16[2048,256]{1,0:T(8,128)(2,1)}, bf16[2048,256]{1,0:T(8,128)(2,1)S(1)}, u32[]{:S(2)}, u32[]{:S(2)}) collective-permute-start(bf16[2048,256]{1,0:T(8,128)(2,1)} %collective-permute-done.1.refs_1_), channel_id=1, source_target_pairs={{0,8},{1,9},{2,10},{3,11},{4,12},{5,13},{6,14},{7,15},{8,0},{9,1},... | collective-permute-start | bytes 3145736 | tf_op jit(solution)/shard_map/ppermute | solution.py:33
  61.9 13.9 %collective-permute-start.6 = (bf16[2048,256]{1,0:T(8,128)(2,1)S(1)}, bf16[2048,256]{1,0:T(8,128)(2,1)S(1)}, u32[]{:S(2)}, u32[]{:S(2)}) collective-permute-start(bf16[2048,256]{1,0:T(8,128)(2,1)S(1)} %collective-permute-done.4.refs_4_), channel_id=1, source_target_pairs={{0,3},{1,0},{2,1},{3,2},{4,7},{5,4},{6,5},{7,6},{8,56},{9,57},{10,... | collective-permute-start | bytes 3145736 | tf_op jit(solution)/shard_map/ppermute | solution.py:33
  62.6 17.1 %collective-permute-start.5 = (bf16[2048,256]{1,0:T(8,128)(2,1)S(1)}, bf16[2048,256]{1,0:T(8,128)(2,1)S(1)}, u32[]{:S(2)}, u32[]{:S(2)}) collective-permute-start(bf16[2048,256]{1,0:T(8,128)(2,1)S(1)} %collective-permute-done.4.refs_4_), channel_id=1, source_target_pairs={{0,1},{1,2},{2,3},{3,0},{4,5},{5,6},{6,7},{7,4},{8,24},{9,25},{10,... | collective-permute-start | bytes 3145736 | tf_op jit(solution)/shard_map/ppermute | solution.py:33
  63.4 6.7 %collective-permute-start.17 = (bf16[1024,256]{1,0:T(8,128)(2,1)S(1)}, bf16[1024,256]{1,0:T(8,128)(2,1)S(1)}, u32[]{:S(2)}, u32[]{:S(2)}) collective-permute-start(bf16[1024,256]{1,0:T(8,128)(2,1)S(1)} %collective-permute-done.8.refs_8_), channel_id=1, source_target_pairs={{0,8},{1,9},{2,10},{3,11},{4,12},{5,13},{6,14},{7,15},{8,0},{9,1},... | collective-permute-start | bytes 1572872 | tf_op jit(solution)/shard_map/ppermute | solution.py:33
  68.5 3.0 %collective-permute-start.16 = (bf16[1024,256]{1,0:T(8,128)(2,1)S(1)}, bf16[1024,256]{1,0:T(8,128)(2,1)S(1)}, u32[]{:S(2)}, u32[]{:S(2)}) collective-permute-start(bf16[1024,256]{1,0:T(8,128)(2,1)S(1)} %collective-permute-done.7.refs_7_), channel_id=1, source_target_pairs={{0,8},{1,9},{2,10},{3,11},{4,12},{5,13},{6,14},{7,15},{8,0},{9,1},... | collective-permute-start | bytes 1572872 | tf_op jit(solution)/shard_map/ppermute | solution.py:33
  70.1 9.7 %collective-permute-start.12 = (bf16[2048,256]{1,0:T(8,128)(2,1)S(1)}, bf16[2048,256]{1,0:T(8,128)(2,1)S(1)}, u32[]{:S(2)}, u32[]{:S(2)}) collective-permute-start(bf16[2048,256]{1,0:T(8,128)(2,1)S(1)} %collective-permute-done.3.refs_3_), channel_id=1, source_target_pairs={{0,8},{1,9},{2,10},{3,11},{4,12},{5,13},{6,14},{7,15},{8,0},{9,1},... | collective-permute-start | bytes 3145736 | tf_op jit(solution)/shard_map/ppermute | solution.py:33
  71.5 8.2 %collective-permute-start.13 = (bf16[2048,256]{1,0:T(8,128)(2,1)S(1)}, bf16[2048,256]{1,0:T(8,128)(2,1)S(1)}, u32[]{:S(2)}, u32[]{:S(2)}) collective-permute-start(bf16[2048,256]{1,0:T(8,128)(2,1)S(1)} %collective-permute-done.4.refs_4_), channel_id=1, source_target_pairs={{0,8},{1,9},{2,10},{3,11},{4,12},{5,13},{6,14},{7,15},{8,0},{9,1},... | collective-permute-start | bytes 3145736 | tf_op jit(solution)/shard_map/ppermute | solution.py:33
  71.9 7.8 %collective-permute-start.11 = (bf16[2048,256]{1,0:T(8,128)(2,1)}, bf16[2048,256]{1,0:T(8,128)(2,1)S(1)}, u32[]{:S(2)}, u32[]{:S(2)}) collective-permute-start(bf16[2048,256]{1,0:T(8,128)(2,1)} %collective-permute-done.2.refs_2_), channel_id=1, source_target_pairs={{0,8},{1,9},{2,10},{3,11},{4,12},{5,13},{6,14},{7,15},{8,0},{9,1},... | collective-permute-start | bytes 3145736 | tf_op jit(solution)/shard_map/ppermute | solution.py:33
  75.9 6.1 %collective-permute-start.15 = (bf16[2048,256]{1,0:T(8,128)(2,1)S(1)}, bf16[2048,256]{1,0:T(8,128)(2,1)S(1)}, u32[]{:S(2)}, u32[]{:S(2)}) collective-permute-start(bf16[2048,256]{1,0:T(8,128)(2,1)S(1)} %collective-permute-done.6.refs_6_), channel_id=1, source_target_pairs={{0,8},{1,9},{2,10},{3,11},{4,12},{5,13},{6,14},{7,15},{8,0},{9,1},... | collective-permute-start | bytes 3145736 | tf_op jit(solution)/shard_map/ppermute | solution.py:33
  79.7 3.8 %collective-permute-start.14 = (bf16[2048,256]{1,0:T(8,128)(2,1)S(1)}, bf16[2048,256]{1,0:T(8,128)(2,1)S(1)}, u32[]{:S(2)}, u32[]{:S(2)}) collective-permute-start(bf16[2048,256]{1,0:T(8,128)(2,1)S(1)} %collective-permute-done.5.refs_5_), channel_id=1, source_target_pairs={{0,8},{1,9},{2,10},{3,11},{4,12},{5,13},{6,14},{7,15},{8,0},{9,1},... | collective-permute-start | bytes 3145736 | tf_op jit(solution)/shard_map/ppermute | solution.py:33

commit v4 on v3

v4 whole, which is shorter than its diff:
```python
import jax
import jax.numpy as jnp
from jax import lax
from jax.experimental import pallas as pl
from jax.experimental.pallas import tpu as pltpu
from jax.sharding import Mesh, PartitionSpec as P

ALL = ("xh", "z", "c", "xl", "y")
SIZES = (2, 4, 2, 2, 4)
ROWS = 1000
COLUMNS = 2000
GROUP = 8
OWN = 16
PAIRS = GROUP * GROUP * 2 * OWN
BLOCK = GROUP * 2 * OWN
PADDED = 2048
PANEL = 256
PANELS = PADDED // PANEL
HALF = 1024
WIDTH = 2
STEPS = PANELS // WIDTH


def device(xh, z, c, xl, y):
    return (((xh % 2 * 4 + z % 4) * 2 + c) * 2 + xl % 2) * 4 + y % 4


def every():
    return [(xh, z, c, xl, y) for xh in range(2) for z in range(4) for c in range(2) for xl in range(2) for y in range(4)]


def move(value, to):
    return lax.ppermute(value, ALL, [(device(*d), device(*to(*d))) for d in every()])


def swap_cores(value):
    return move(value, lambda xh, z, c, xl, y: (xh, z, 1 - c, xl, y))


def swap_x(value):
    return move(value, lambda xh, z, c, xl, y: (xh, z, c, xl + 1, y) if c == 0 else (xh + 1, z, c, xl, y))


def ring(value, by):
    return move(value, lambda xh, z, c, xl, y: (xh, z, c, xl, y + by) if c == 0 else (xh, z + by, c, xl, y))


def spread(table):
    rows = -(-table.shape[0] // 1024) * 8
    return jnp.pad(table, (0, rows * 128 - table.shape[0])).reshape(rows, 128)


def weights_kernel(valence_ref, conduction_ref, val_ref, cond_ref, omegas_ref, out_ref):
    def lookup(index, table):
        high, low = index // 128, index % 128
        block = lax.broadcasted_iota(jnp.int32, (table.shape[0], PAIRS), 0)
        picked = lax.dot_general(
            table,
            (block == high).astype(jnp.float32),
            (((0,), (0,)), ((), ())),
            precision=lax.Precision.HIGHEST,
            preferred_element_type=jnp.float32,
        )
        lane = lax.broadcasted_iota(jnp.int32, (128, PAIRS), 0)
        return jnp.sum(jnp.where(lane == low, picked, 0.0), axis=0, keepdims=True)

    gap = lookup(conduction_ref[...], cond_ref[...]) - lookup(valence_ref[...], val_ref[...])
    for f in range(2):
        omega = omegas_ref[f]
        out_ref[f : f + 1, :] = -4.0 * gap / (gap * gap + omega * omega)


VMEM = pl.BlockSpec(memory_space=pltpu.VMEM)
ANY = pl.BlockSpec(memory_space=pl.ANY)
SMEM = pl.BlockSpec(memory_space=pltpu.SMEM)


def pair_weights(valence_index, conduction_index, val_energy, cond_energy, omegas):
    def order(index):
        return index.reshape(GROUP, 2, GROUP, OWN).transpose(2, 0, 1, 3).reshape(1, PAIRS)

    return pl.pallas_call(
        weights_kernel,
        out_shape=jax.ShapeDtypeStruct((2, PAIRS), jnp.float32),
        in_specs=[VMEM] * 4 + [SMEM],
        out_specs=VMEM,
        compiler_params=pltpu.CompilerParams(vmem_limit_bytes=24 << 20),
        name="weights",
    )(order(valence_index), order(conduction_index), spread(val_energy), spread(cond_energy), omegas)


def slices_kernel(which_ref, in_ref, *refs):
    out_ref = refs[-1]
    which = which_ref[0]
    for s in range(GROUP):
        out_ref[s, which, :, :COLUMNS] = in_ref[:, s * COLUMNS : (s + 1) * COLUMNS]
    out_ref[:, which, :, COLUMNS:] = jnp.zeros((GROUP, OWN, PADDED - COLUMNS), jnp.bfloat16)


def slices(which, pairs, *part):
    return pl.pallas_call(
        slices_kernel,
        out_shape=jax.ShapeDtypeStruct((GROUP, 2, OWN, PADDED), jnp.bfloat16),
        in_specs=[SMEM, VMEM] + [VMEM] * len(part),
        out_specs=VMEM,
        input_output_aliases={2: 0} if part else {},
        compiler_params=pltpu.CompilerParams(vmem_limit_bytes=16 << 20),
        name="slices",
    )(which, pairs, *part)


def turn_kernel(core_ref, in_ref, out_ref):
    @pl.when(core_ref[0] == 0)
    def _():
        for half in range(2):
            part = in_ref[:, half * ROWS : (half + 1) * ROWS]
            part = jnp.concatenate([part, jnp.zeros((BLOCK, HALF - ROWS), jnp.bfloat16)], axis=1)
            out_ref[half * HALF : (half + 1) * HALF, :] = part.T

    @pl.when(core_ref[0] == 1)
    def _():
        for p in range(PANELS):
            out_ref[p * BLOCK : (p + 1) * BLOCK, :] = in_ref[:, p * PANEL : (p + 1) * PANEL]


def turn(core, value):
    return pl.pallas_call(
        turn_kernel,
        out_shape=jax.ShapeDtypeStruct((PADDED, BLOCK), jnp.bfloat16),
        in_specs=[SMEM, VMEM],
        out_specs=VMEM,
        compiler_params=pltpu.CompilerParams(vmem_limit_bytes=16 << 20),
        name="turn",
    )(core, value)


RING = (0, 3, 1, 2)
NEAR = len(RING)
LANES = NEAR * 2 * OWN
NEAR_PAIRS = NEAR * LANES
LATE_PAIRS = PAIRS - NEAR_PAIRS


class Meta:
    def __init__(self, ref):
        self.core, self.xl, self.xh = ref[0], ref[1], ref[2]
        self.row = [ref[3 + k] for k in range(NEAR)]
        self.column = [ref[3 + NEAR + k] for k in range(NEAR)]


def half_of(refs, k, which):
    if k == GROUP - 1:
        return refs[k + which]
    return refs[k].at[pl.ds(which * HALF, HALF)]


def column_part(refs, k, step, x):
    which, part = divmod(step, STEPS // 2)
    ref = half_of(refs, k, which).at[pl.ds(part * WIDTH * BLOCK, WIDTH * BLOCK)]
    return ref.reshape(WIDTH, GROUP, 2 * OWN, PANEL).at[:, pl.ds(x * NEAR, NEAR)]


def panels(step):
    return pl.ds(step * WIDTH, WIDTH)


def by_core(meta, mine, theirs, run):
    @pl.when(meta.core == 0)
    def _():
        run(mine, theirs, 0)

    @pl.when(meta.core == 1)
    def _():
        run(theirs, mine, 1)


def scale(rows, y, x_row, x_column, weight_ref):
    lanes = pl.ds(pl.multiple_of(x_column * LANES, LANES), LANES)
    part = rows[y, :ROWS, lanes].astype(jnp.float32)
    start = pl.multiple_of((x_row * NEAR + y) * BLOCK + x_column * LANES, LANES)
    return [(part * weight_ref[f : f + 1, pl.ds(start, LANES)]).astype(jnp.bfloat16) for f in range(2)]


def early_kernel(meta_ref, weight_ref, *refs):
    mine, theirs = refs[:NEAR], refs[NEAR : 2 * NEAR]
    out_ref, next_ref, rows, scaled, columns, rows_sem, columns_sem = refs[2 * NEAR :]
    j = pl.program_id(0)
    meta = Meta(meta_ref)

    def row_copy(k, refs, core):
        return pltpu.make_async_copy(half_of(refs, k, core), rows.at[meta.row[k]], rows_sem.at[k])

    def column_copy(k, step, refs):
        to = columns.at[panels(step), :, meta.column[k]]
        return pltpu.make_async_copy(column_part(refs, k, step, meta.xl), to, columns_sem.at[step, k])

    @pl.when(j == 0)
    def _():
        def start(row_refs, column_refs, core):
            for k in range(NEAR):
                row_copy(k, row_refs, core).start()
            for step in range(STEPS):
                for k in range(NEAR):
                    column_copy(k, step, column_refs).start()

        by_core(meta, mine, theirs, start)
        for k in range(NEAR):
            row_copy(k, mine, 0).wait()
        for y in range(NEAR):
            lanes = slice(y * LANES, (y + 1) * LANES)
            for f, value in enumerate(scale(rows, y, meta.xl, meta.xh, weight_ref)):
                scaled[f, :, lanes] = value
            for f, value in enumerate(scale(rows, y, meta.xl, 1 - meta.xh, weight_ref)):
                next_ref[f, :, lanes] = value

    for step in range(STEPS):

        @pl.when(j == step)
        def _(step=step):
            for k in range(NEAR):
                column_copy(k, step, mine).wait()

    for panel in range(WIDTH):
        right = columns[j * WIDTH + panel].reshape(NEAR_PAIRS, PANEL)
        for f in range(2):
            out_ref[panel, f] = jnp.dot(scaled[f], right, preferred_element_type=jnp.float32)


def cost(pairs, size):
    return pl.CostEstimate(flops=4 * ROWS * COLUMNS * pairs, bytes_accessed=size, transcendentals=0)


def early_product(meta, weight, mine, theirs):
    return pl.pallas_call(
        early_kernel,
        grid=(STEPS,),
        out_shape=(
            pltpu.HBM((PANELS, 2, ROWS, PANEL), jnp.float32),
            jax.ShapeDtypeStruct((2, ROWS, NEAR_PAIRS), jnp.bfloat16),
        ),
        in_specs=[SMEM, VMEM] + [ANY] * (2 * NEAR),
        out_specs=(
            pl.BlockSpec((WIDTH, 2, ROWS, PANEL), lambda j: (j, 0, 0, 0)),
            pl.BlockSpec((2, ROWS, NEAR_PAIRS), lambda j: (0, 0, 0)),
        ),
        scratch_shapes=[
            pltpu.VMEM((NEAR, HALF, BLOCK), jnp.bfloat16),
            pltpu.VMEM((2, ROWS, NEAR_PAIRS), jnp.bfloat16),
            pltpu.VMEM((PANELS, NEAR, NEAR, 2 * OWN, PANEL), jnp.bfloat16),
            pltpu.SemaphoreType.DMA((NEAR,)),
            pltpu.SemaphoreType.DMA((STEPS, NEAR)),
        ],
        compiler_params=pltpu.CompilerParams(vmem_limit_bytes=24 << 20),
        name="early_product",
    )(meta, weight, *mine, *theirs)


def late_kernel(meta_ref, weight_ref, sum_ref, next_ref, *refs):
    count = GROUP + 1
    mine, theirs = refs[:count], refs[count : 2 * count]
    out_ref, rows, scaled, columns, sums, rows_sem, columns_sem, sums_sem, next_sem = refs[2 * count :]
    j = pl.program_id(0)
    meta = Meta(meta_ref)

    def row_copy(k, refs, core):
        return pltpu.make_async_copy(half_of(refs, NEAR + k, core), rows.at[meta.row[k]], rows_sem.at[k])

    def column_copies(step, refs):
        copies = []
        for k in range(GROUP):
            beside, place = k // NEAR, meta.column[k % NEAR]
            to = columns.at[panels(step), pl.ds((1 + beside) * NEAR, NEAR), place]
            part = column_part(refs, k, step, 1 - meta.xl)
            copies.append(pltpu.make_async_copy(part, to, columns_sem.at[step, k]))
            if beside:
                to = columns.at[panels(step), pl.ds(0, NEAR), place]
                part = column_part(refs, k, step, meta.xl)
                copies.append(pltpu.make_async_copy(part, to, columns_sem.at[step, NEAR + k]))
        return copies

    def sum_copy(step):
        return pltpu.make_async_copy(sum_ref.at[panels(step)], sums, sums_sem)

    next_copy = pltpu.make_async_copy(next_ref, scaled.at[:, :, pl.ds(0, NEAR_PAIRS)], next_sem)

    def step_dot(step, panel, f, pairs):
        right = columns[step * WIDTH + panel].reshape(LATE_PAIRS, PANEL)[pairs]
        return jnp.dot(scaled[f, :, pairs], right, preferred_element_type=jnp.float32)

    for step in range(STEPS):

        @pl.when(j == step)
        def _(step=step):
            if step == 0:

                def start_first(row_refs, column_refs, core):
                    for k in range(NEAR):
                        row_copy(k, row_refs, core).start()
                    next_copy.start()
                    for copy in column_copies(0, column_refs):
                        copy.start()

                def start_rest(row_refs, column_refs, core):
                    for step in range(1, STEPS):
                        for copy in column_copies(step, column_refs):
                            copy.start()

                by_core(meta, mine, theirs, start_first)
                for k in range(NEAR):
                    row_copy(k, mine, 0).wait()
                next_copy.wait()
                sum_copy(0).start()
                by_core(meta, mine, theirs, start_rest)
            for copy in column_copies(step, mine):
                copy.wait()
            lanes = [slice(panel * PANEL, (panel + 1) * PANEL) for panel in range(WIDTH)]
            if step == 0:
                for panel in range(WIDTH):
                    for f in range(2):
                        out_ref[f, :, lanes[panel]] = step_dot(0, panel, f, slice(0, NEAR_PAIRS))
                for y in range(NEAR):
                    for beside in range(2):
                        first = ((1 + beside) * NEAR + y) * LANES
                        x_column = meta.xh if beside == 0 else 1 - meta.xh
                        for f, value in enumerate(scale(rows, y, 1 - meta.xl, x_column, weight_ref)):
                            scaled[f, :, first : first + LANES] = value
            sum_copy(step).wait()
            for panel in range(WIDTH):
                for f in range(2):
                    total = sums[panel, f]
                    if step == 0:
                        total = total + out_ref[f, :, lanes[panel]]
                    pairs = slice(NEAR_PAIRS if step == 0 else 0, LATE_PAIRS)
                    out_ref[f, :, lanes[panel]] = total + step_dot(step, panel, f, pairs)
            if step + 1 < STEPS:
                sum_copy(step + 1).start()


def late_product(meta, weight, total, following, mine, theirs):
    return pl.pallas_call(
        late_kernel,
        grid=(STEPS,),
        out_shape=jax.ShapeDtypeStruct((2, ROWS, COLUMNS), jnp.float32),
        in_specs=[SMEM, VMEM] + [ANY] * (2 * GROUP + 4),
        out_specs=pl.BlockSpec((2, ROWS, WIDTH * PANEL), lambda j: (0, 0, j)),
        scratch_shapes=[
            pltpu.VMEM((NEAR, HALF, BLOCK), jnp.bfloat16),
            pltpu.VMEM((2, ROWS, LATE_PAIRS), jnp.bfloat16),
            pltpu.VMEM((PANELS, 3 * NEAR, NEAR, 2 * OWN, PANEL), jnp.bfloat16),
            pltpu.VMEM((WIDTH, 2, ROWS, PANEL), jnp.float32),
            pltpu.SemaphoreType.DMA((NEAR,)),
            pltpu.SemaphoreType.DMA((STEPS, GROUP + NEAR)),
            pltpu.SemaphoreType.DMA,
            pltpu.SemaphoreType.DMA,
        ],
        compiler_params=pltpu.CompilerParams(vmem_limit_bytes=32 << 20),
        cost_estimate=cost(LATE_PAIRS, 48 << 20),
        name="late_product",
    )(meta, weight, total, following, *mine, *theirs)


def exchange(value):
    wide = [[device(a // 4, a % 4, 0, xl, y) for a in range(GROUP)] for xl in range(2) for y in range(4)]
    narrow = [[device(xh, z, 1, b // 4, b % 4) for b in range(GROUP)] for xh in range(2) for z in range(4)]
    return lax.all_to_all(value, ALL, 0, 0, axis_index_groups=wide + narrow, tiled=True)


def describe():
    def around(axis):
        return [(lax.axis_index(axis) + shift) % NEAR for shift in RING]

    own = [lax.axis_index(axis) for axis in ("c", "xl", "xh")]
    return jnp.stack(own + around("y") + around("z")).astype(jnp.int32)


def body(pair_elements, valence_index, conduction_index, val_energy, cond_energy, omegas):
    core = lax.axis_index("c").astype(jnp.int32)[None]
    meta = describe()
    part = slices(1 - core, swap_cores(pair_elements), slices(core, pair_elements))
    part = exchange(part)
    own = turn(core, part.reshape(BLOCK, PADDED))
    weight = pair_weights(valence_index, conduction_index, val_energy, cond_energy, omegas)
    near = [ring(own, by) for by in (1, -1, 2)]
    beside = swap_x(own)
    near, beside, weight, meta = lax.optimization_barrier((near, beside, weight, meta))
    late = [ring(beside, by) for by in (1, -1)]
    far = [swap_x(near[2][:HALF]), ring(beside[HALF:], 2)]
    mine = [own] + near
    theirs = [swap_cores(v) for v in mine]
    total, following = early_product(meta, weight, mine, theirs)
    beside, far, total = lax.optimization_barrier((beside, far, total))
    others = [swap_cores(v) for v in [beside] + far]
    late, others = lax.optimization_barrier((late, others))
    mine += [beside] + late + far
    theirs += [others[0]] + [swap_cores(v) for v in late] + others[1:]
    return late_product(meta, weight, total, following, mine, theirs)


def solution(mesh):
    fine = Mesh(mesh.devices.reshape(SIZES), ALL)
    wide, narrow = ("xh", "z", "c"), ("xl", "y")
    return jax.shard_map(
        body,
        mesh=fine,
        in_specs=(P(wide + narrow, None), P(), P(), P(), P(), P()),
        out_specs=P(None, wide, narrow),
        check_vma=False,
    )
```

time: 108 us -> 116 us (1.074)
  Pallas kernels: 26.5 us -> 42.9 us
  starting transfers between devices: 35.2 us -> 26.2 us
    pallas_call x1 -> x2, Pallas kernels: 23.7 us -> 40.1 us  [the longest x1 29.8 us: late_product(): pl.pallas_call(late_kernel, grid=(STEPS,), out_shape=jax.ShapeDtypeStruct...]
    ppermute x18, starting transfers between devices: 35.2 us -> 26.2 us  [move(): lax.ppermute(value, ALL, [(device(*d), device(*to(*d))) for d in every()])]
  transfers between devices with their start and end apart: 18 -> 18, of which waited for: 8 -> 7; matrix products, arithmetic and copies ran while one was open for 3% -> 4% of each run, Pallas kernels for 2% -> 11%
where the time goes in v4:
time: 116 us; the launch traced here: 115 us
  Pallas kernels  42.9 us (37%)
  starting transfers between devices  26.2 us (23%)
  waiting for transfers between devices  21.1 us (18%)
  blocking collectives  18.1 us (16%)
  local copies, waits for them, and re-layouts  6.27 us (5%)
    pallas_call x1, Pallas kernels, late_product(): pl.pallas_call(late_kernel, grid=(STEPS,), out_shape=jax.ShapeDtypeStruct...  29.8 us
    ppermute x18, starting transfers between devices, move(): lax.ppermute(value, ALL, [(device(*d), device(*to(*d))) for d in every()])  26.2 us
    ppermute x18, waiting for transfers between devices, move(): lax.ppermute(value, ALL, [(device(*d), device(*to(*d))) for d in every()])  21.1 us
    all_to_all x1, blocking collectives, exchange(): lax.all_to_all(value, ALL, 0, 0, axis_index_groups=wide + narrow, tiled=T...  18.1 us
    pallas_call x1, Pallas kernels, early_product(): pl.pallas_call(early_kernel, grid=(STEPS,), out_shape=(pltpu.HBM((PANELS,...  10.3 us
    pallas_call x1, Pallas kernels, pair_weights(): pl.pallas_call(weights_kernel, out_shape=jax.ShapeDtypeStruct((2, PAIRS),...  2.42 us
  transfers between devices with their start and end apart: 18, of which 7 were waited for; matrix products, arithmetic and copies ran while one was open for 4% of the time, Pallas kernels for 11%

profile of v4, /device:TPU:1, one launch (start us, length us, event | category | flops | bytes accessed | tf_op | source)
XLA Modules:
  0.0 114.9 jit_solution(13590034028449460235)
XLA Ops:
  0.0 1.4 %collective-permute-start = (bf16[16,16000]{1,0:T(8,128)(2,1)}, bf16[16,16000]{1,0:T(8,128)(2,1)S(1)}, u32[]{:S(2)}, u32[]{:S(2)}) collective-permute-start(bf16[16,16000]{1,0:T(8,128)(2,1)} %in_ref.1), channel_id=1, source_target_pairs={{0,8},{1,9},{2,10},{3,11},{4,12},{5,13},{6,14},{7,15},{8,0},{9,1},... | collective-permute-start | bytes 1536008 | tf_op jit(solution)/shard_map/ppermute | solution.py:33
  1.4 0.0 copy-start
  1.4 1.0 copy-done
  2.5 0.2 slices.2.refs_0_
  2.7 0.5 collective-permute-done.in_ref
  3.2 0.2 slices.3
  3.4 18.1 %all_to_all.5 = bf16[8,2,16,2048]{3,2,1,0:T(8,128)(2,1)S(1)} all-to-all(bf16[8,2,16,2048]{3,2,1,0:T(8,128)(2,1)S(1)} %slices.3), channel_id=1, replica_groups={{0,16,32,48,64,80,96,112},{1,17,33,49,65,81,97,113},{2,18,34,50,66,82,9..., dimensions={0} | all-to-all | bytes 2097152 | tf_op jit(solution)/shard_map/all_to_all | solution.py:365
  21.4 0.1 turn.1.refs_0_
  21.5 1.1 collective-permute-start.4
  22.6 4.3 %collective-permute-start.3 = (bf16[2048,256]{1,0:T(8,128)(2,1)S(1)}, bf16[2048,256]{1,0:T(8,128)(2,1)S(1)}, u32[]{:S(2)}, u32[]{:S(2)}) collective-permute-start(bf16[2048,256]{1,0:T(8,128)(2,1)S(1)} %turn.1.refs_0_), channel_id=1, source_target_pairs={{0,2},{1,3},{2,0},{3,1},{4,6},{5,7},{6,4},{7,5},{8,40},{9,41},{10,... | collective-permute-start | bytes 3145736 | tf_op jit(solution)/shard_map/ppermute | solution.py:33
  27.0 0.5 collective-permute-start.2
  27.5 0.9 collective-permute-start.1
  28.4 5.4 %collective-permute-start.7 = (bf16[2048,256]{1,0:T(8,128)(2,1)S(1)}, bf16[2048,256]{1,0:T(8,128)(2,1)}, u32[]{:S(2)}, u32[]{:S(2)}) collective-permute-start(bf16[2048,256]{1,0:T(8,128)(2,1)S(1)} %turn.1.refs_0_), channel_id=1, source_target_pairs={{0,8},{1,9},{2,10},{3,11},{4,12},{5,13},{6,14},{7,15},{8,0},{9,1},... | collective-permute-start | bytes 3145736 | tf_op jit(solution)/shard_map/ppermute | solution.py:33
  33.8 0.8 reshape.22
  34.6 0.1 reshape.23.valence_ref
  34.7 0.8 reshape.24
  35.6 0.1 reshape.25.conduction_ref
  35.8 0.7 pad_bitcast_fusion.1.val_ref
  36.5 0.8 pad_bitcast_fusion.cond_ref
  37.3 0.0 copy-start.1
  37.3 0.7 copy-done.1
  37.9 2.4 %weights.1.weight_ref = f32[2,2048]{1,0:T(2,128)S(1)} custom-call(s32[1,2048]{1,0:T(1,128)S(1)} %reshape.23.valence_ref, s32[1,2048]{1,0:T(1,128)S(1)} %reshape.25.conduction_ref, f32[24,128]{1,0:T(8,128)S(1)} %pad_bitcast_fusion.1.val_ref, f32[80,128]{1,0:T(8,128)S(1)} %pad_bitcast_fusion.cond_ref, f32[2]{0:T(128)S(1)} %copy-done.1), custom_call_target="tpu_custom_call" | custom-call | tf_op jit(solution)/shard_map/weights/pallas_call | solution.py:82
  40.4 0.1 stack.44.meta_ref
  40.4 1.7 %collective-permute-done.4.refs_4_ = bf16[2048,256]{1,0:T(8,128)(2,1)} collective-permute-done((bf16[2048,256]{1,0:T(8,128)(2,1)S(1)}, bf16[2048,256]{1,0:T(8,128)(2,1)}, u32[]{:S(2)}, u32[]{:S(2)}) %collective-permute-start.4) | collective-permute-done | bytes 1048608 | tf_op jit(solution)/shard_map/ppermute | solution.py:33
  42.1 0.0 collective-permute-done.3.refs_3_
  42.1 9.8 %collective-permute-done.2.refs_2_ = bf16[2048,256]{1,0:T(8,128)(2,1)S(1)} collective-permute-done((bf16[2048,256]{1,0:T(8,128)(2,1)S(1)}, bf16[2048,256]{1,0:T(8,128)(2,1)S(1)}, u32[]{:S(2)}, u32[]{:S(2)}) %collective-permute-start.2) | collective-permute-done | bytes 1048608 | tf_op jit(solution)/shard_map/ppermute | solution.py:33
  51.9 0.0 collective-permute-done.1.refs_1_
  51.9 4.5 %collective-permute-start.8 = (bf16[2048,256]{1,0:T(8,128)(2,1)}, bf16[2048,256]{1,0:T(8,128)(2,1)S(1)}, u32[]{:S(2)}, u32[]{:S(2)}) collective-permute-start(bf16[2048,256]{1,0:T(8,128)(2,1)} %collective-permute-done.1.refs_1_), channel_id=1, source_target_pairs={{0,8},{1,9},{2,10},{3,11},{4,12},{5,13},{6,14},{7,15},{8,0},{9,1},... | collective-permute-start | bytes 3145736 | tf_op jit(solution)/shard_map/ppermute | solution.py:33
  56.4 0.0 collective-permute-start.9
  56.4 0.5 collective-permute-start.10
  56.9 1.1 slice.7
  58.0 1.9 %collective-permute-start.5 = (bf16[1024,256]{1,0:T(8,128)(2,1)S(1)}, bf16[1024,256]{1,0:T(8,128)(2,1)S(1)}, u32[]{:S(2)}, u32[]{:S(2)}) collective-permute-start(bf16[1024,256]{1,0:T(8,128)(2,1)S(1)} %slice.6), channel_id=1, source_target_pairs={{0,4},{1,5},{2,6},{3,7},{4,0},{5,1},{6,2},{7,3},{8,72},{9,73},{10,... | collective-permute-start | bytes 1572872 | tf_op jit(solution)/shard_map/ppermute | solution.py:33
  59.9 0.0 collective-permute-done.7.refs_4_.refs_9_
  59.9 0.4 collective-permute-start.6
  60.3 0.0 collective-permute-done.8.refs_5_.refs_10_
  60.3 2.1 %collective-permute-start.12 = (bf16[2048,256]{1,0:T(8,128)(2,1)}, bf16[2048,256]{1,0:T(8,128)(2,1)S(1)}, u32[]{:S(2)}, u32[]{:S(2)}) collective-permute-start(bf16[2048,256]{1,0:T(8,128)(2,1)} %collective-permute-done.4.refs_4_), channel_id=1, source_target_pairs={{0,3},{1,0},{2,1},{3,2},{4,7},{5,4},{6,5},{7,6},{8,56},{9,57},{10,... | collective-permute-start | bytes 3145736 | tf_op jit(solution)/shard_map/ppermute | solution.py:33
  62.4 0.0 collective-permute-done.9.refs_6_.refs_11_
  62.4 0.0 collective-permute-start.11
  62.4 0.0 collective-permute-done.10.refs_7_.refs_12_
  62.5 10.3 %early_product.1 = (f32[8,2,1000,256]{3,2,1,0:T(8,128)}, bf16[2,1000,512]{2,1,0:T(8,128)(2,1)S(1)}) custom-call(s32[11]{0:T(128)S(1)} %stack.44.meta_ref, f32[2,2048]{1,0:T(2,128)S(1)} %weights.1.weight_ref, bf16[2048,256]{1,0:T(8,128)(2,1)S(1)} %turn.1.refs_0_, bf16[2048,256]{1,0:T(8,128)(2,1)} %collective-permute-done.1.refs_1_, ...), custom_call_target="tpu_custom_call" | custom-call | tf_op jit(solution)/shard_map/early_product/pallas_call | solution.py:234
  72.8 0.0 collective-permute-done.5.refs_7_
  72.8 0.0 collective-permute-done.6.refs_8_
  72.8 1.9 %collective-permute-start.13 = (bf16[2048,256]{1,0:T(8,128)(2,1)}, bf16[2048,256]{1,0:T(8,128)(2,1)S(1)}, u32[]{:S(2)}, u32[]{:S(2)}) collective-permute-start(bf16[2048,256]{1,0:T(8,128)(2,1)} %collective-permute-done.4.refs_4_), channel_id=1, source_target_pairs={{0,8},{1,9},{2,10},{3,11},{4,12},{5,13},{6,14},{7,15},{8,0},{9,1},... | collective-permute-start | bytes 3145736 | tf_op jit(solution)/shard_map/ppermute | solution.py:33
  74.7 0.1 collective-permute-start.14
  74.7 0.4 collective-permute-start.15
  75.2 4.0 %collective-permute-done.12.refs_6_ = bf16[2048,256]{1,0:T(8,128)(2,1)S(1)} collective-permute-done((bf16[2048,256]{1,0:T(8,128)(2,1)}, bf16[2048,256]{1,0:T(8,128)(2,1)S(1)}, u32[]{:S(2)}, u32[]{:S(2)}) %collective-permute-start.12) | collective-permute-done | bytes 1048608 | tf_op jit(solution)/shard_map/ppermute | solution.py:33
  79.2 1.6 %collective-permute-done.11.refs_5_ = bf16[2048,256]{1,0:T(8,128)(2,1)S(1)} collective-permute-done((bf16[2048,256]{1,0:T(8,128)(2,1)}, bf16[2048,256]{1,0:T(8,128)(2,1)S(1)}, u32[]{:S(2)}, u32[]{:S(2)}) %collective-permute-start.11) | collective-permute-done | bytes 1048608 | tf_op jit(solution)/shard_map/ppermute | solution.py:33
  80.7 0.0 collective-permute-done.14.refs_16_
  80.7 0.0 collective-permute-done.15.refs_17_
  80.7 0.0 collective-permute-done.13.refs_13_
  80.7 0.5 collective-permute-start.16
  81.2 0.3 collective-permute-start.17
  81.5 2.0 %collective-permute-done.16.refs_14_ = bf16[2048,256]{1,0:T(8,128)(2,1)S(1)} collective-permute-done((bf16[2048,256]{1,0:T(8,128)(2,1)S(1)}, bf16[2048,256]{1,0:T(8,128)(2,1)S(1)}, u32[]{:S(2)}, u32[]{:S(2)}) %collective-permute-start.16) | collective-permute-done | bytes 1048608 | tf_op jit(solution)/shard_map/ppermute | solution.py:33
  83.5 1.5 %collective-permute-done.17.refs_15_ = bf16[2048,256]{1,0:T(8,128)(2,1)S(1)} collective-permute-done((bf16[2048,256]{1,0:T(8,128)(2,1)S(1)}, bf16[2048,256]{1,0:T(8,128)(2,1)S(1)}, u32[]{:S(2)}, u32[]{:S(2)}) %collective-permute-start.17) | collective-permute-done | bytes 1048608 | tf_op jit(solution)/shard_map/ppermute | solution.py:33
  85.0 29.8 %late_product.1 = f32[2,1000,2000]{2,1,0:T(8,128)} custom-call(s32[11]{0:T(128)S(1)} %stack.44.meta_ref, f32[2,2048]{1,0:T(2,128)S(1)} %weights.1.weight_ref, f32[8,2,1000,256]{3,2,1,0:T(8,128)} %get-tuple-element.29.sum_ref, bf16[2,1000,512]{2,1,0:T(8,128)(2,1)S(1)} %get-tuple-element.30.next_ref, bf16[2048,256]{1,0:T(8,128)(2,1)S(1)} %turn.1.refs_0_, ...), custom_call_target="tpu_custom_call" | custom-call | flops 12288000000 | bytes 50331648 | tf_op jit(solution)/shard_map/late_product/pallas_call | solution.py:340
  (3 shorter events, 0.1 us)
Async XLA Ops:
  0.0 3.2 %collective-permute-start = (bf16[16,16000]{1,0:T(8,128)(2,1)}, bf16[16,16000]{1,0:T(8,128)(2,1)S(1)}, u32[]{:S(2)}, u32[]{:S(2)}) collective-permute-start(bf16[16,16000]{1,0:T(8,128)(2,1)} %in_ref.1), channel_id=1, source_target_pairs={{0,8},{1,9},{2,10},{3,11},{4,12},{5,13},{6,14},{7,15},{8,0},{9,1},... | collective-permute-start | bytes 1536008 | tf_op jit(solution)/shard_map/ppermute | solution.py:33
  1.4 1.0 copy-start
  21.5 20.6 %collective-permute-start.4 = (bf16[2048,256]{1,0:T(8,128)(2,1)S(1)}, bf16[2048,256]{1,0:T(8,128)(2,1)}, u32[]{:S(2)}, u32[]{:S(2)}) collective-permute-start(bf16[2048,256]{1,0:T(8,128)(2,1)S(1)} %turn.1.refs_0_), channel_id=1, source_target_pairs={{0,4},{1,5},{2,6},{3,7},{4,0},{5,1},{6,2},{7,3},{8,72},{9,73},{10,... | collective-permute-start | bytes 3145736 | tf_op jit(solution)/shard_map/ppermute | solution.py:33
  22.6 19.5 %collective-permute-start.3 = (bf16[2048,256]{1,0:T(8,128)(2,1)S(1)}, bf16[2048,256]{1,0:T(8,128)(2,1)S(1)}, u32[]{:S(2)}, u32[]{:S(2)}) collective-permute-start(bf16[2048,256]{1,0:T(8,128)(2,1)S(1)} %turn.1.refs_0_), channel_id=1, source_target_pairs={{0,2},{1,3},{2,0},{3,1},{4,6},{5,7},{6,4},{7,5},{8,40},{9,41},{10,... | collective-permute-start | bytes 3145736 | tf_op jit(solution)/shard_map/ppermute | solution.py:33
  27.0 25.0 %collective-permute-start.2 = (bf16[2048,256]{1,0:T(8,128)(2,1)S(1)}, bf16[2048,256]{1,0:T(8,128)(2,1)S(1)}, u32[]{:S(2)}, u32[]{:S(2)}) collective-permute-start(bf16[2048,256]{1,0:T(8,128)(2,1)S(1)} %turn.1.refs_0_), channel_id=1, source_target_pairs={{0,3},{1,0},{2,1},{3,2},{4,7},{5,4},{6,5},{7,6},{8,56},{9,57},{10,... | collective-permute-start | bytes 3145736 | tf_op jit(solution)/shard_map/ppermute | solution.py:33
  27.5 24.4 %collective-permute-start.1 = (bf16[2048,256]{1,0:T(8,128)(2,1)S(1)}, bf16[2048,256]{1,0:T(8,128)(2,1)}, u32[]{:S(2)}, u32[]{:S(2)}) collective-permute-start(bf16[2048,256]{1,0:T(8,128)(2,1)S(1)} %turn.1.refs_0_), channel_id=1, source_target_pairs={{0,1},{1,2},{2,3},{3,0},{4,5},{5,6},{6,7},{7,4},{8,24},{9,25},{10,... | collective-permute-start | bytes 3145736 | tf_op jit(solution)/shard_map/ppermute | solution.py:33
  28.4 31.5 %collective-permute-start.7 = (bf16[2048,256]{1,0:T(8,128)(2,1)S(1)}, bf16[2048,256]{1,0:T(8,128)(2,1)}, u32[]{:S(2)}, u32[]{:S(2)}) collective-permute-start(bf16[2048,256]{1,0:T(8,128)(2,1)S(1)} %turn.1.refs_0_), channel_id=1, source_target_pairs={{0,8},{1,9},{2,10},{3,11},{4,12},{5,13},{6,14},{7,15},{8,0},{9,1},... | collective-permute-start | bytes 3145736 | tf_op jit(solution)/shard_map/ppermute | solution.py:33
  37.3 0.7 copy-start.1
  51.9 8.4 %collective-permute-start.8 = (bf16[2048,256]{1,0:T(8,128)(2,1)}, bf16[2048,256]{1,0:T(8,128)(2,1)S(1)}, u32[]{:S(2)}, u32[]{:S(2)}) collective-permute-start(bf16[2048,256]{1,0:T(8,128)(2,1)} %collective-permute-done.1.refs_1_), channel_id=1, source_target_pairs={{0,8},{1,9},{2,10},{3,11},{4,12},{5,13},{6,14},{7,15},{8,0},{9,1},... | collective-permute-start | bytes 3145736 | tf_op jit(solution)/shard_map/ppermute | solution.py:33
  56.4 6.1 %collective-permute-start.9 = (bf16[2048,256]{1,0:T(8,128)(2,1)S(1)}, bf16[2048,256]{1,0:T(8,128)(2,1)S(1)}, u32[]{:S(2)}, u32[]{:S(2)}) collective-permute-start(bf16[2048,256]{1,0:T(8,128)(2,1)S(1)} %collective-permute-done.2.refs_2_), channel_id=1, source_target_pairs={{0,8},{1,9},{2,10},{3,11},{4,12},{5,13},{6,14},{7,15},{8,0},{9,1},... | collective-permute-start | bytes 3145736 | tf_op jit(solution)/shard_map/ppermute | solution.py:33
  56.4 6.1 %collective-permute-start.10 = (bf16[2048,256]{1,0:T(8,128)(2,1)S(1)}, bf16[2048,256]{1,0:T(8,128)(2,1)S(1)}, u32[]{:S(2)}, u32[]{:S(2)}) collective-permute-start(bf16[2048,256]{1,0:T(8,128)(2,1)S(1)} %collective-permute-done.3.refs_3_), channel_id=1, source_target_pairs={{0,8},{1,9},{2,10},{3,11},{4,12},{5,13},{6,14},{7,15},{8,0},{9,1},... | collective-permute-start | bytes 3145736 | tf_op jit(solution)/shard_map/ppermute | solution.py:33
  58.0 14.8 %collective-permute-start.5 = (bf16[1024,256]{1,0:T(8,128)(2,1)S(1)}, bf16[1024,256]{1,0:T(8,128)(2,1)S(1)}, u32[]{:S(2)}, u32[]{:S(2)}) collective-permute-start(bf16[1024,256]{1,0:T(8,128)(2,1)S(1)} %slice.6), channel_id=1, source_target_pairs={{0,4},{1,5},{2,6},{3,7},{4,0},{5,1},{6,2},{7,3},{8,72},{9,73},{10,... | collective-permute-start | bytes 1572872 | tf_op jit(solution)/shard_map/ppermute | solution.py:33
  59.9 12.9 %collective-permute-start.6 = (bf16[1024,256]{1,0:T(8,128)(2,1)S(1)}, bf16[1024,256]{1,0:T(8,128)(2,1)S(1)}, u32[]{:S(2)}, u32[]{:S(2)}) collective-permute-start(bf16[1024,256]{1,0:T(8,128)(2,1)S(1)} %slice.7), channel_id=1, source_target_pairs={{0,2},{1,3},{2,0},{3,1},{4,6},{5,7},{6,4},{7,5},{8,40},{9,41},{10,... | collective-permute-start | bytes 1572872 | tf_op jit(solution)/shard_map/ppermute | solution.py:33
  60.3 18.8 %collective-permute-start.12 = (bf16[2048,256]{1,0:T(8,128)(2,1)}, bf16[2048,256]{1,0:T(8,128)(2,1)S(1)}, u32[]{:S(2)}, u32[]{:S(2)}) collective-permute-start(bf16[2048,256]{1,0:T(8,128)(2,1)} %collective-permute-done.4.refs_4_), channel_id=1, source_target_pairs={{0,3},{1,0},{2,1},{3,2},{4,7},{5,4},{6,5},{7,6},{8,56},{9,57},{10,... | collective-permute-start | bytes 3145736 | tf_op jit(solution)/shard_map/ppermute | solution.py:33
  62.4 18.3 %collective-permute-start.11 = (bf16[2048,256]{1,0:T(8,128)(2,1)}, bf16[2048,256]{1,0:T(8,128)(2,1)S(1)}, u32[]{:S(2)}, u32[]{:S(2)}) collective-permute-start(bf16[2048,256]{1,0:T(8,128)(2,1)} %collective-permute-done.4.refs_4_), channel_id=1, source_target_pairs={{0,1},{1,2},{2,3},{3,0},{4,5},{5,6},{6,7},{7,4},{8,24},{9,25},{10,... | collective-permute-start | bytes 3145736 | tf_op jit(solution)/shard_map/ppermute | solution.py:33
  72.8 8.0 %collective-permute-start.13 = (bf16[2048,256]{1,0:T(8,128)(2,1)}, bf16[2048,256]{1,0:T(8,128)(2,1)S(1)}, u32[]{:S(2)}, u32[]{:S(2)}) collective-permute-start(bf16[2048,256]{1,0:T(8,128)(2,1)} %collective-permute-done.4.refs_4_), channel_id=1, source_target_pairs={{0,8},{1,9},{2,10},{3,11},{4,12},{5,13},{6,14},{7,15},{8,0},{9,1},... | collective-permute-start | bytes 3145736 | tf_op jit(solution)/shard_map/ppermute | solution.py:33
  74.7 6.1 %collective-permute-start.14 = (bf16[1024,256]{1,0:T(8,128)(2,1)S(1)}, bf16[1024,256]{1,0:T(8,128)(2,1)S(1)}, u32[]{:S(2)}, u32[]{:S(2)}) collective-permute-start(bf16[1024,256]{1,0:T(8,128)(2,1)S(1)} %collective-permute-done.5.refs_7_), channel_id=1, source_target_pairs={{0,8},{1,9},{2,10},{3,11},{4,12},{5,13},{6,14},{7,15},{8,0},{9,1},... | collective-permute-start | bytes 1572872 | tf_op jit(solution)/shard_map/ppermute | solution.py:33
  74.7 6.0 %collective-permute-start.15 = (bf16[1024,256]{1,0:T(8,128)(2,1)S(1)}, bf16[1024,256]{1,0:T(8,128)(2,1)S(1)}, u32[]{:S(2)}, u32[]{:S(2)}) collective-permute-start(bf16[1024,256]{1,0:T(8,128)(2,1)S(1)} %collective-permute-done.6.refs_8_), channel_id=1, source_target_pairs={{0,8},{1,9},{2,10},{3,11},{4,12},{5,13},{6,14},{7,15},{8,0},{9,1},... | collective-permute-start | bytes 1572872 | tf_op jit(solution)/shard_map/ppermute | solution.py:33
  80.7 2.8 %collective-permute-start.16 = (bf16[2048,256]{1,0:T(8,128)(2,1)S(1)}, bf16[2048,256]{1,0:T(8,128)(2,1)S(1)}, u32[]{:S(2)}, u32[]{:S(2)}) collective-permute-start(bf16[2048,256]{1,0:T(8,128)(2,1)S(1)} %collective-permute-done.11.refs_5_), channel_id=1, source_target_pairs={{0,8},{1,9},{2,10},{3,11},{4,12},{5,13},{6,14},{7,15},{8,0},{9,1},... | collective-permute-start | bytes 3145736 | tf_op jit(solution)/shard_map/ppermute | solution.py:33
  81.2 3.8 %collective-permute-start.17 = (bf16[2048,256]{1,0:T(8,128)(2,1)S(1)}, bf16[2048,256]{1,0:T(8,128)(2,1)S(1)}, u32[]{:S(2)}, u32[]{:S(2)}) collective-permute-start(bf16[2048,256]{1,0:T(8,128)(2,1)S(1)} %collective-permute-done.12.refs_6_), channel_id=1, source_target_pairs={{0,8},{1,9},{2,10},{3,11},{4,12},{5,13},{6,14},{7,15},{8,0},{9,1},... | collective-permute-start | bytes 3145736 | tf_op jit(solution)/shard_map/ppermute | solution.py:33

commit v5 on v4

--- a/solution.py
+++ b/solution.py
@@ -279,7 +279,7 @@
         return copies
 
     def sum_copy(step):
-        return pltpu.make_async_copy(sum_ref.at[panels(step)], sums, sums_sem)
+        return pltpu.make_async_copy(sum_ref.at[panels(step)], sums.at[step % 2], sums_sem.at[step % 2])
 
     next_copy = pltpu.make_async_copy(next_ref, scaled.at[:, :, pl.ds(0, NEAR_PAIRS)], next_sem)
 
@@ -313,6 +313,8 @@
                 by_core(meta, mine, theirs, start_rest)
             for copy in column_copies(step, mine):
                 copy.wait()
+            if step + 1 < STEPS:
+                sum_copy(step + 1).start()
             lanes = [slice(panel * PANEL, (panel + 1) * PANEL) for panel in range(WIDTH)]
             if step == 0:
                 for panel in range(WIDTH):
@@ -327,13 +329,11 @@
             sum_copy(step).wait()
             for panel in range(WIDTH):
                 for f in range(2):
-                    total = sums[panel, f]
+                    total = sums[step % 2, panel, f]
                     if step == 0:
                         total = total + out_ref[f, :, lanes[panel]]
                     pairs = slice(NEAR_PAIRS if step == 0 else 0, LATE_PAIRS)
                     out_ref[f, :, lanes[panel]] = total + step_dot(step, panel, f, pairs)
-            if step + 1 < STEPS:
-                sum_copy(step + 1).start()
 
 
 def late_product(meta, weight, total, following, mine, theirs):
@@ -347,13 +347,13 @@
             pltpu.VMEM((NEAR, HALF, BLOCK), jnp.bfloat16),
             pltpu.VMEM((2, ROWS, LATE_PAIRS), jnp.bfloat16),
             pltpu.VMEM((PANELS, 3 * NEAR, NEAR, 2 * OWN, PANEL), jnp.bfloat16),
-            pltpu.VMEM((WIDTH, 2, ROWS, PANEL), jnp.float32),
+            pltpu.VMEM((2, WIDTH, 2, ROWS, PANEL), jnp.float32),
             pltpu.SemaphoreType.DMA((NEAR,)),
             pltpu.SemaphoreType.DMA((STEPS, GROUP + NEAR)),
-            pltpu.SemaphoreType.DMA,
+            pltpu.SemaphoreType.DMA((2,)),
             pltpu.SemaphoreType.DMA,
         ],
-        compiler_params=pltpu.CompilerParams(vmem_limit_bytes=32 << 20),
+        compiler_params=pltpu.CompilerParams(vmem_limit_bytes=36 << 20),
         cost_estimate=cost(LATE_PAIRS, 48 << 20),
         name="late_product",
     )(meta, weight, total, following, *mine, *theirs)

time: 116 us -> 106 us (0.914)
  Pallas kernels: 42.9 us -> 33.7 us
  local copies, waits for them, and re-layouts: 6.27 us -> 7.59 us
  waiting for transfers between devices: 21.1 us -> 19.9 us
    pallas_call x1, Pallas kernels: 29.8 us -> 20.5 us  [late_product(): pl.pallas_call(late_kernel, grid=(STEPS,), out_shape=jax.ShapeDtypeStruct...]
    unnamed x4 -> x6, local copies, waits for them, and re-layouts: 1.69 us -> 3.01 us
    ppermute x18, waiting for transfers between devices: 21.1 us -> 19.9 us  [move(): lax.ppermute(value, ALL, [(device(*d), device(*to(*d))) for d in every()])]
  transfers between devices with their start and end apart: 18 -> 18, of which waited for: 7 -> 7; matrix products, arithmetic and copies ran while one was open for 4% -> 4% of each run, Pallas kernels for 11% -> 12%
where the time goes in v5:
time: 106 us
  Pallas kernels  33.7 us (32%)
  starting transfers between devices  26.1 us (25%)
  waiting for transfers between devices  19.9 us (19%)
  blocking collectives  18.1 us (17%)
  local copies, waits for them, and re-layouts  7.59 us (7%)
    ppermute x18, starting transfers between devices, move(): lax.ppermute(value, ALL, [(device(*d), device(*to(*d))) for d in every()])  26.1 us
    pallas_call x1, Pallas kernels, late_product(): pl.pallas_call(late_kernel, grid=(STEPS,), out_shape=jax.ShapeDtypeStruct...  20.5 us
    ppermute x18, waiting for transfers between devices, move(): lax.ppermute(value, ALL, [(device(*d), device(*to(*d))) for d in every()])  19.9 us
    all_to_all x1, blocking collectives, exchange(): lax.all_to_all(value, ALL, 0, 0, axis_index_groups=wide + narrow, tiled=T...  18.1 us
    pallas_call x1, Pallas kernels, early_product(): pl.pallas_call(early_kernel, grid=(STEPS,), out_shape=(pltpu.HBM((PANELS,...  10.3 us
    unnamed x6, local copies, waits for them, and re-layouts  3.01 us
    pallas_call x1, Pallas kernels, pair_weights(): pl.pallas_call(weights_kernel, out_shape=jax.ShapeDtypeStruct((2, PAIRS),...  2.42 us
  transfers between devices with their start and end apart: 18, of which 7 were waited for; matrix products, arithmetic and copies ran while one was open for 4% of the time, Pallas kernels for 12%

profile of v5, /device:TPU:1, one launch (start us, length us, event | category | flops | bytes accessed | tf_op | source)
XLA Modules:
  0.0 105.7 jit_solution(17879211629903518862)
XLA Ops:
  0.0 1.4 %collective-permute-start = (bf16[16,16000]{1,0:T(8,128)(2,1)}, bf16[16,16000]{1,0:T(8,128)(2,1)S(1)}, u32[]{:S(2)}, u32[]{:S(2)}) collective-permute-start(bf16[16,16000]{1,0:T(8,128)(2,1)} %in_ref.1), channel_id=1, source_target_pairs={{0,8},{1,9},{2,10},{3,11},{4,12},{5,13},{6,14},{7,15},{8,0},{9,1},... | collective-permute-start | bytes 1536008 | tf_op jit(solution)/shard_map/ppermute | solution.py:33
  1.4 0.0 copy-start.1
  1.4 1.0 copy-done.1
  2.5 0.2 slices.2.refs_0_
  2.7 0.5 collective-permute-done.in_ref
  3.2 0.2 slices.3
  3.4 18.1 %all_to_all.5 = bf16[8,2,16,2048]{3,2,1,0:T(8,128)(2,1)S(1)} all-to-all(bf16[8,2,16,2048]{3,2,1,0:T(8,128)(2,1)S(1)} %slices.3), channel_id=1, replica_groups={{0,16,32,48,64,80,96,112},{1,17,33,49,65,81,97,113},{2,18,34,50,66,82,9..., dimensions={0} | all-to-all | bytes 2097152 | tf_op jit(solution)/shard_map/all_to_all | solution.py:365
  21.4 0.1 turn.1.refs_0_
  21.5 1.1 %collective-permute-start.4 = (bf16[2048,256]{1,0:T(8,128)(2,1)S(1)}, bf16[2048,256]{1,0:T(8,128)(2,1)}, u32[]{:S(2)}, u32[]{:S(2)}) collective-permute-start(bf16[2048,256]{1,0:T(8,128)(2,1)S(1)} %turn.1.refs_0_), channel_id=1, source_target_pairs={{0,4},{1,5},{2,6},{3,7},{4,0},{5,1},{6,2},{7,3},{8,72},{9,73},{10,... | collective-permute-start | bytes 3145736 | tf_op jit(solution)/shard_map/ppermute | solution.py:33
  22.6 4.3 %collective-permute-start.3 = (bf16[2048,256]{1,0:T(8,128)(2,1)S(1)}, bf16[2048,256]{1,0:T(8,128)(2,1)S(1)}, u32[]{:S(2)}, u32[]{:S(2)}) collective-permute-start(bf16[2048,256]{1,0:T(8,128)(2,1)S(1)} %turn.1.refs_0_), channel_id=1, source_target_pairs={{0,2},{1,3},{2,0},{3,1},{4,6},{5,7},{6,4},{7,5},{8,40},{9,41},{10,... | collective-permute-start | bytes 3145736 | tf_op jit(solution)/shard_map/ppermute | solution.py:33
  27.0 0.5 collective-permute-start.2
  27.5 0.9 collective-permute-start.1
  28.4 5.4 %collective-permute-start.7 = (bf16[2048,256]{1,0:T(8,128)(2,1)S(1)}, bf16[2048,256]{1,0:T(8,128)(2,1)}, u32[]{:S(2)}, u32[]{:S(2)}) collective-permute-start(bf16[2048,256]{1,0:T(8,128)(2,1)S(1)} %turn.1.refs_0_), channel_id=1, source_target_pairs={{0,8},{1,9},{2,10},{3,11},{4,12},{5,13},{6,14},{7,15},{8,0},{9,1},... | collective-permute-start | bytes 3145736 | tf_op jit(solution)/shard_map/ppermute | solution.py:33
  33.8 0.8 reshape.22
  34.6 0.1 reshape.23.valence_ref
  34.7 0.8 reshape.24
  35.6 0.1 reshape.25.conduction_ref
  35.8 0.7 pad_bitcast_fusion.1.val_ref
  36.5 0.8 pad_bitcast_fusion.cond_ref
  37.3 0.0 copy-start.2
  37.3 0.7 copy-done.2
  37.9 2.4 %weights.1.weight_ref = f32[2,2048]{1,0:T(2,128)S(1)} custom-call(s32[1,2048]{1,0:T(1,128)S(1)} %reshape.23.valence_ref, s32[1,2048]{1,0:T(1,128)S(1)} %reshape.25.conduction_ref, f32[24,128]{1,0:T(8,128)S(1)} %pad_bitcast_fusion.1.val_ref, f32[80,128]{1,0:T(8,128)S(1)} %pad_bitcast_fusion.cond_ref, f32[2]{0:T(128)S(1)} %copy-done.2), custom_call_target="tpu_custom_call" | custom-call | tf_op jit(solution)/shard_map/weights/pallas_call | solution.py:82
  40.4 0.1 stack.44.meta_ref
  40.4 1.7 %collective-permute-done.4.refs_4_ = bf16[2048,256]{1,0:T(8,128)(2,1)} collective-permute-done((bf16[2048,256]{1,0:T(8,128)(2,1)S(1)}, bf16[2048,256]{1,0:T(8,128)(2,1)}, u32[]{:S(2)}, u32[]{:S(2)}) %collective-permute-start.4) | collective-permute-done | bytes 1048608 | tf_op jit(solution)/shard_map/ppermute | solution.py:33
  42.1 0.0 collective-permute-done.3.refs_3_
  42.1 9.8 %collective-permute-done.2.refs_2_ = bf16[2048,256]{1,0:T(8,128)(2,1)S(1)} collective-permute-done((bf16[2048,256]{1,0:T(8,128)(2,1)S(1)}, bf16[2048,256]{1,0:T(8,128)(2,1)S(1)}, u32[]{:S(2)}, u32[]{:S(2)}) %collective-permute-start.2) | collective-permute-done | bytes 1048608 | tf_op jit(solution)/shard_map/ppermute | solution.py:33
  51.9 0.0 collective-permute-done.1.refs_1_
  51.9 4.5 %collective-permute-start.8 = (bf16[2048,256]{1,0:T(8,128)(2,1)}, bf16[2048,256]{1,0:T(8,128)(2,1)S(1)}, u32[]{:S(2)}, u32[]{:S(2)}) collective-permute-start(bf16[2048,256]{1,0:T(8,128)(2,1)} %collective-permute-done.1.refs_1_), channel_id=1, source_target_pairs={{0,8},{1,9},{2,10},{3,11},{4,12},{5,13},{6,14},{7,15},{8,0},{9,1},... | collective-permute-start | bytes 3145736 | tf_op jit(solution)/shard_map/ppermute | solution.py:33
  56.4 0.0 collective-permute-start.9
  56.4 0.5 collective-permute-start.10
  56.9 1.1 %slice.7 = bf16[1024,256]{1,0:T(8,128)(2,1)S(1)} slice(bf16[2048,256]{1,0:T(8,128)(2,1)} %collective-permute-done.4.refs_4_), slice={[1024:2048], [0:256]} | slice | bytes 1048576 | tf_op jit(solution)/shard_map/slice | solution.py:387
  58.0 1.9 %collective-permute-start.5 = (bf16[1024,256]{1,0:T(8,128)(2,1)S(1)}, bf16[1024,256]{1,0:T(8,128)(2,1)S(1)}, u32[]{:S(2)}, u32[]{:S(2)}) collective-permute-start(bf16[1024,256]{1,0:T(8,128)(2,1)S(1)} %slice.6), channel_id=1, source_target_pairs={{0,4},{1,5},{2,6},{3,7},{4,0},{5,1},{6,2},{7,3},{8,72},{9,73},{10,... | collective-permute-start | bytes 1572872 | tf_op jit(solution)/shard_map/ppermute | solution.py:33
  59.9 0.0 collective-permute-done.7.refs_4_.refs_9_
  59.9 0.4 collective-permute-start.6
  60.3 0.0 collective-permute-done.8.refs_5_.refs_10_
  60.3 2.1 %collective-permute-start.12 = (bf16[2048,256]{1,0:T(8,128)(2,1)}, bf16[2048,256]{1,0:T(8,128)(2,1)S(1)}, u32[]{:S(2)}, u32[]{:S(2)}) collective-permute-start(bf16[2048,256]{1,0:T(8,128)(2,1)} %collective-permute-done.4.refs_4_), channel_id=1, source_target_pairs={{0,3},{1,0},{2,1},{3,2},{4,7},{5,4},{6,5},{7,6},{8,56},{9,57},{10,... | collective-permute-start | bytes 3145736 | tf_op jit(solution)/shard_map/ppermute | solution.py:33
  62.4 0.0 collective-permute-done.9.refs_6_.refs_11_
  62.4 0.0 collective-permute-start.11
  62.4 0.0 collective-permute-done.10.refs_7_.refs_12_
  62.5 10.3 %early_product.1 = (f32[8,2,1000,256]{3,2,1,0:T(8,128)}, bf16[2,1000,512]{2,1,0:T(8,128)(2,1)S(1)}) custom-call(s32[11]{0:T(128)S(1)} %stack.44.meta_ref, f32[2,2048]{1,0:T(2,128)S(1)} %weights.1.weight_ref, bf16[2048,256]{1,0:T(8,128)(2,1)S(1)} %turn.1.refs_0_, bf16[2048,256]{1,0:T(8,128)(2,1)} %collective-permute-done.1.refs_1_, ...), custom_call_target="tpu_custom_call" | custom-call | tf_op jit(solution)/shard_map/early_product/pallas_call | solution.py:234
  72.7 0.0 copy-start
  72.8 1.3 %copy-done = bf16[2,1000,512]{2,1,0:T(8,128)(2,1)} copy-done((bf16[2,1000,512]{2,1,0:T(8,128)(2,1)}, bf16[2,1000,512]{2,1,0:T(8,128)(2,1)S(1)}, u32[]{:S(2)}) %copy-start) | copy-done | bytes 2048024
  74.1 0.0 collective-permute-done.5.refs_7_
  74.1 0.0 collective-permute-done.6.refs_8_
  74.1 1.8 %collective-permute-start.13 = (bf16[2048,256]{1,0:T(8,128)(2,1)}, bf16[2048,256]{1,0:T(8,128)(2,1)S(1)}, u32[]{:S(2)}, u32[]{:S(2)}) collective-permute-start(bf16[2048,256]{1,0:T(8,128)(2,1)} %collective-permute-done.4.refs_4_), channel_id=1, source_target_pairs={{0,8},{1,9},{2,10},{3,11},{4,12},{5,13},{6,14},{7,15},{8,0},{9,1},... | collective-permute-start | bytes 3145736 | tf_op jit(solution)/shard_map/ppermute | solution.py:33
  75.9 0.1 collective-permute-start.14
  76.0 0.4 collective-permute-start.15
  76.4 2.8 %collective-permute-done.12.refs_6_ = bf16[2048,256]{1,0:T(8,128)(2,1)S(1)} collective-permute-done((bf16[2048,256]{1,0:T(8,128)(2,1)}, bf16[2048,256]{1,0:T(8,128)(2,1)S(1)}, u32[]{:S(2)}, u32[]{:S(2)}) %collective-permute-start.12) | collective-permute-done | bytes 1048608 | tf_op jit(solution)/shard_map/ppermute | solution.py:33
  79.2 1.6 %collective-permute-done.11.refs_5_ = bf16[2048,256]{1,0:T(8,128)(2,1)S(1)} collective-permute-done((bf16[2048,256]{1,0:T(8,128)(2,1)}, bf16[2048,256]{1,0:T(8,128)(2,1)S(1)}, u32[]{:S(2)}, u32[]{:S(2)}) %collective-permute-start.11) | collective-permute-done | bytes 1048608 | tf_op jit(solution)/shard_map/ppermute | solution.py:33
  80.7 0.0 collective-permute-done.14.refs_16_
  80.7 0.0 collective-permute-done.15.refs_17_
  80.7 0.0 collective-permute-done.13.refs_13_
  80.7 0.5 collective-permute-start.16
  81.2 0.3 collective-permute-start.17
  81.5 2.0 %collective-permute-done.16.refs_14_ = bf16[2048,256]{1,0:T(8,128)(2,1)S(1)} collective-permute-done((bf16[2048,256]{1,0:T(8,128)(2,1)S(1)}, bf16[2048,256]{1,0:T(8,128)(2,1)S(1)}, u32[]{:S(2)}, u32[]{:S(2)}) %collective-permute-start.16) | collective-permute-done | bytes 1048608 | tf_op jit(solution)/shard_map/ppermute | solution.py:33
  83.5 1.5 %collective-permute-done.17.refs_15_ = bf16[2048,256]{1,0:T(8,128)(2,1)S(1)} collective-permute-done((bf16[2048,256]{1,0:T(8,128)(2,1)S(1)}, bf16[2048,256]{1,0:T(8,128)(2,1)S(1)}, u32[]{:S(2)}, u32[]{:S(2)}) %collective-permute-start.17) | collective-permute-done | bytes 1048608 | tf_op jit(solution)/shard_map/ppermute | solution.py:33
  85.0 20.5 %late_product.1 = f32[2,1000,2000]{2,1,0:T(8,128)} custom-call(s32[11]{0:T(128)S(1)} %stack.44.meta_ref, f32[2,2048]{1,0:T(2,128)S(1)} %weights.1.weight_ref, f32[8,2,1000,256]{3,2,1,0:T(8,128)} %get-tuple-element.29.sum_ref, bf16[2,1000,512]{2,1,0:T(8,128)(2,1)} %copy-done, bf16[2048,256]{1,0:T(8,128)(2,1)S(1)} %turn.1.refs_0_, ...), custom_call_target="tpu_custom_call" | custom-call | flops 12288000000 | bytes 50331648 | tf_op jit(solution)/shard_map/late_product/pallas_call | solution.py:340
  (3 shorter events, 0.1 us)
Async XLA Ops:
  0.0 3.2 %collective-permute-start = (bf16[16,16000]{1,0:T(8,128)(2,1)}, bf16[16,16000]{1,0:T(8,128)(2,1)S(1)}, u32[]{:S(2)}, u32[]{:S(2)}) collective-permute-start(bf16[16,16000]{1,0:T(8,128)(2,1)} %in_ref.1), channel_id=1, source_target_pairs={{0,8},{1,9},{2,10},{3,11},{4,12},{5,13},{6,14},{7,15},{8,0},{9,1},... | collective-permute-start | bytes 1536008 | tf_op jit(solution)/shard_map/ppermute | solution.py:33
  1.4 1.0 copy-start.1
  21.5 20.6 %collective-permute-start.4 = (bf16[2048,256]{1,0:T(8,128)(2,1)S(1)}, bf16[2048,256]{1,0:T(8,128)(2,1)}, u32[]{:S(2)}, u32[]{:S(2)}) collective-permute-start(bf16[2048,256]{1,0:T(8,128)(2,1)S(1)} %turn.1.refs_0_), channel_id=1, source_target_pairs={{0,4},{1,5},{2,6},{3,7},{4,0},{5,1},{6,2},{7,3},{8,72},{9,73},{10,... | collective-permute-start | bytes 3145736 | tf_op jit(solution)/shard_map/ppermute | solution.py:33
  22.6 19.5 %collective-permute-start.3 = (bf16[2048,256]{1,0:T(8,128)(2,1)S(1)}, bf16[2048,256]{1,0:T(8,128)(2,1)S(1)}, u32[]{:S(2)}, u32[]{:S(2)}) collective-permute-start(bf16[2048,256]{1,0:T(8,128)(2,1)S(1)} %turn.1.refs_0_), channel_id=1, source_target_pairs={{0,2},{1,3},{2,0},{3,1},{4,6},{5,7},{6,4},{7,5},{8,40},{9,41},{10,... | collective-permute-start | bytes 3145736 | tf_op jit(solution)/shard_map/ppermute | solution.py:33
  27.0 25.0 %collective-permute-start.2 = (bf16[2048,256]{1,0:T(8,128)(2,1)S(1)}, bf16[2048,256]{1,0:T(8,128)(2,1)S(1)}, u32[]{:S(2)}, u32[]{:S(2)}) collective-permute-start(bf16[2048,256]{1,0:T(8,128)(2,1)S(1)} %turn.1.refs_0_), channel_id=1, source_target_pairs={{0,3},{1,0},{2,1},{3,2},{4,7},{5,4},{6,5},{7,6},{8,56},{9,57},{10,... | collective-permute-start | bytes 3145736 | tf_op jit(solution)/shard_map/ppermute | solution.py:33
  27.5 24.4 %collective-permute-start.1 = (bf16[2048,256]{1,0:T(8,128)(2,1)S(1)}, bf16[2048,256]{1,0:T(8,128)(2,1)}, u32[]{:S(2)}, u32[]{:S(2)}) collective-permute-start(bf16[2048,256]{1,0:T(8,128)(2,1)S(1)} %turn.1.refs_0_), channel_id=1, source_target_pairs={{0,1},{1,2},{2,3},{3,0},{4,5},{5,6},{6,7},{7,4},{8,24},{9,25},{10,... | collective-permute-start | bytes 3145736 | tf_op jit(solution)/shard_map/ppermute | solution.py:33
  28.4 31.5 %collective-permute-start.7 = (bf16[2048,256]{1,0:T(8,128)(2,1)S(1)}, bf16[2048,256]{1,0:T(8,128)(2,1)}, u32[]{:S(2)}, u32[]{:S(2)}) collective-permute-start(bf16[2048,256]{1,0:T(8,128)(2,1)S(1)} %turn.1.refs_0_), channel_id=1, source_target_pairs={{0,8},{1,9},{2,10},{3,11},{4,12},{5,13},{6,14},{7,15},{8,0},{9,1},... | collective-permute-start | bytes 3145736 | tf_op jit(solution)/shard_map/ppermute | solution.py:33
  37.3 0.7 copy-start.2
  51.9 8.4 %collective-permute-start.8 = (bf16[2048,256]{1,0:T(8,128)(2,1)}, bf16[2048,256]{1,0:T(8,128)(2,1)S(1)}, u32[]{:S(2)}, u32[]{:S(2)}) collective-permute-start(bf16[2048,256]{1,0:T(8,128)(2,1)} %collective-permute-done.1.refs_1_), channel_id=1, source_target_pairs={{0,8},{1,9},{2,10},{3,11},{4,12},{5,13},{6,14},{7,15},{8,0},{9,1},... | collective-permute-start | bytes 3145736 | tf_op jit(solution)/shard_map/ppermute | solution.py:33
  56.4 6.1 %collective-permute-start.9 = (bf16[2048,256]{1,0:T(8,128)(2,1)S(1)}, bf16[2048,256]{1,0:T(8,128)(2,1)S(1)}, u32[]{:S(2)}, u32[]{:S(2)}) collective-permute-start(bf16[2048,256]{1,0:T(8,128)(2,1)S(1)} %collective-permute-done.2.refs_2_), channel_id=1, source_target_pairs={{0,8},{1,9},{2,10},{3,11},{4,12},{5,13},{6,14},{7,15},{8,0},{9,1},... | collective-permute-start | bytes 3145736 | tf_op jit(solution)/shard_map/ppermute | solution.py:33
  56.4 6.1 %collective-permute-start.10 = (bf16[2048,256]{1,0:T(8,128)(2,1)S(1)}, bf16[2048,256]{1,0:T(8,128)(2,1)S(1)}, u32[]{:S(2)}, u32[]{:S(2)}) collective-permute-start(bf16[2048,256]{1,0:T(8,128)(2,1)S(1)} %collective-permute-done.3.refs_3_), channel_id=1, source_target_pairs={{0,8},{1,9},{2,10},{3,11},{4,12},{5,13},{6,14},{7,15},{8,0},{9,1},... | collective-permute-start | bytes 3145736 | tf_op jit(solution)/shard_map/ppermute | solution.py:33
  58.0 16.1 %collective-permute-start.5 = (bf16[1024,256]{1,0:T(8,128)(2,1)S(1)}, bf16[1024,256]{1,0:T(8,128)(2,1)S(1)}, u32[]{:S(2)}, u32[]{:S(2)}) collective-permute-start(bf16[1024,256]{1,0:T(8,128)(2,1)S(1)} %slice.6), channel_id=1, source_target_pairs={{0,4},{1,5},{2,6},{3,7},{4,0},{5,1},{6,2},{7,3},{8,72},{9,73},{10,... | collective-permute-start | bytes 1572872 | tf_op jit(solution)/shard_map/ppermute | solution.py:33
  59.9 14.2 %collective-permute-start.6 = (bf16[1024,256]{1,0:T(8,128)(2,1)S(1)}, bf16[1024,256]{1,0:T(8,128)(2,1)S(1)}, u32[]{:S(2)}, u32[]{:S(2)}) collective-permute-start(bf16[1024,256]{1,0:T(8,128)(2,1)S(1)} %slice.7), channel_id=1, source_target_pairs={{0,2},{1,3},{2,0},{3,1},{4,6},{5,7},{6,4},{7,5},{8,40},{9,41},{10,... | collective-permute-start | bytes 1572872 | tf_op jit(solution)/shard_map/ppermute | solution.py:33
  60.3 18.8 %collective-permute-start.12 = (bf16[2048,256]{1,0:T(8,128)(2,1)}, bf16[2048,256]{1,0:T(8,128)(2,1)S(1)}, u32[]{:S(2)}, u32[]{:S(2)}) collective-permute-start(bf16[2048,256]{1,0:T(8,128)(2,1)} %collective-permute-done.4.refs_4_), channel_id=1, source_target_pairs={{0,3},{1,0},{2,1},{3,2},{4,7},{5,4},{6,5},{7,6},{8,56},{9,57},{10,... | collective-permute-start | bytes 3145736 | tf_op jit(solution)/shard_map/ppermute | solution.py:33
  62.4 18.3 %collective-permute-start.11 = (bf16[2048,256]{1,0:T(8,128)(2,1)}, bf16[2048,256]{1,0:T(8,128)(2,1)S(1)}, u32[]{:S(2)}, u32[]{:S(2)}) collective-permute-start(bf16[2048,256]{1,0:T(8,128)(2,1)} %collective-permute-done.4.refs_4_), channel_id=1, source_target_pairs={{0,1},{1,2},{2,3},{3,0},{4,5},{5,6},{6,7},{7,4},{8,24},{9,25},{10,... | collective-permute-start | bytes 3145736 | tf_op jit(solution)/shard_map/ppermute | solution.py:33
  72.7 1.3 %copy-start = (bf16[2,1000,512]{2,1,0:T(8,128)(2,1)}, bf16[2,1000,512]{2,1,0:T(8,128)(2,1)S(1)}, u32[]{:S(2)}) copy-start(bf16[2,1000,512]{2,1,0:T(8,128)(2,1)S(1)} %get-tuple-element.30.next_ref) | copy-start | bytes 6144004
  74.1 6.7 %collective-permute-start.13 = (bf16[2048,256]{1,0:T(8,128)(2,1)}, bf16[2048,256]{1,0:T(8,128)(2,1)S(1)}, u32[]{:S(2)}, u32[]{:S(2)}) collective-permute-start(bf16[2048,256]{1,0:T(8,128)(2,1)} %collective-permute-done.4.refs_4_), channel_id=1, source_target_pairs={{0,8},{1,9},{2,10},{3,11},{4,12},{5,13},{6,14},{7,15},{8,0},{9,1},... | collective-permute-start | bytes 3145736 | tf_op jit(solution)/shard_map/ppermute | solution.py:33
  75.9 4.9 %collective-permute-start.14 = (bf16[1024,256]{1,0:T(8,128)(2,1)S(1)}, bf16[1024,256]{1,0:T(8,128)(2,1)S(1)}, u32[]{:S(2)}, u32[]{:S(2)}) collective-permute-start(bf16[1024,256]{1,0:T(8,128)(2,1)S(1)} %collective-permute-done.5.refs_7_), channel_id=1, source_target_pairs={{0,8},{1,9},{2,10},{3,11},{4,12},{5,13},{6,14},{7,15},{8,0},{9,1},... | collective-permute-start | bytes 1572872 | tf_op jit(solution)/shard_map/ppermute | solution.py:33
  76.0 4.8 %collective-permute-start.15 = (bf16[1024,256]{1,0:T(8,128)(2,1)S(1)}, bf16[1024,256]{1,0:T(8,128)(2,1)S(1)}, u32[]{:S(2)}, u32[]{:S(2)}) collective-permute-start(bf16[1024,256]{1,0:T(8,128)(2,1)S(1)} %collective-permute-done.6.refs_8_), channel_id=1, source_target_pairs={{0,8},{1,9},{2,10},{3,11},{4,12},{5,13},{6,14},{7,15},{8,0},{9,1},... | collective-permute-start | bytes 1572872 | tf_op jit(solution)/shard_map/ppermute | solution.py:33
  80.7 2.8 %collective-permute-start.16 = (bf16[2048,256]{1,0:T(8,128)(2,1)S(1)}, bf16[2048,256]{1,0:T(8,128)(2,1)S(1)}, u32[]{:S(2)}, u32[]{:S(2)}) collective-permute-start(bf16[2048,256]{1,0:T(8,128)(2,1)S(1)} %collective-permute-done.11.refs_5_), channel_id=1, source_target_pairs={{0,8},{1,9},{2,10},{3,11},{4,12},{5,13},{6,14},{7,15},{8,0},{9,1},... | collective-permute-start | bytes 3145736 | tf_op jit(solution)/shard_map/ppermute | solution.py:33
  81.2 3.8 %collective-permute-start.17 = (bf16[2048,256]{1,0:T(8,128)(2,1)S(1)}, bf16[2048,256]{1,0:T(8,128)(2,1)S(1)}, u32[]{:S(2)}, u32[]{:S(2)}) collective-permute-start(bf16[2048,256]{1,0:T(8,128)(2,1)S(1)} %collective-permute-done.12.refs_6_), channel_id=1, source_target_pairs={{0,8},{1,9},{2,10},{3,11},{4,12},{5,13},{6,14},{7,15},{8,0},{9,1},... | collective-permute-start | bytes 3145736 | tf_op jit(solution)/shard_map/ppermute | solution.py:33
